TPU v7x, 32 devices: a whole 2x2x4 slice. The times are simulated.
32 devices in a mesh: bins: 4 (over y, core), batch: 8 (over z, x).
Axes of the slice: x: 2, y: 2, z: 4, core: 2. Of those that a mesh axis runs over, the one named last changes fastest.
Arguments:
- features: bfloat16 [8, 1024, 1536], P('batch', 'bins'), may hold values from -6 to 6
- norm_gain: float32 [1536], replicated, may hold values from 0.25 to 1.75
- convolution_taps_weight: bfloat16 [3, 1536, 768], replicated, may hold values from -0.09375 to 0.09375
- out_weight: bfloat16 [768, 1536], replicated, may hold values from -0.21875 to 0.21875
- head_weight: bfloat16 [1536, 4096], P(None, 'batch'), may hold values from -0.15625 to 0.15625
- rc_perm: int32 [1536], replicated, may hold values from 0 to 1535, each once
- exon_bins: int32 [8, 16, 8], P('batch'), may hold values from 0 to 1023, as said below
- exon_count: int32 [8, 16], P('batch'), may hold values from 1 to 8
- gene_strand: int32 [8, 16], P('batch'), may hold values 0 or 1
- gene_target: float32 [8, 16, 4096], P('batch', 'bins'), may hold values from 0.5 to 8
Outputs:
- input_grad: bfloat16 [8, 1024, 1536], P('batch', 'bins')
- out_weight_grad: float32 [768, 1536], P('batch')
Inputs may be any that keep to these rules, and one draw needn't show every extreme that they name: `rc_perm`: a permutation of the channels. `exon_bins`: bins of the gene's own sequence; a bin may be listed more than once; each gene's listed bins lie within 256 consecutive bins. All genes of a sequence may lie within the same 256 bins j * 256 to (j + 1) * 256 - 1 of one j, and then every one of those bins may be listed and counted.
All inputs are finite; a program needn't handle non-finite values. No bound on the sum of `gene_strand` on one device may be relied on, other than what follows from the above.
Results may differ from a plain program's by a relative error of at most 0.014.
Values may be sent and summed in bfloat16 or wider, within the bound.
A program may use at most 128 MiB of HBM per device.

v0:
```python
import jax
import jax.numpy as jnp
from jax import lax
from jax.sharding import PartitionSpec as P

DILATION_STEP = 16


def with_halo(block, sides, width):
    for axis, dim in sides:
        count = lax.axis_size(axis)
        forward = [(i, i + 1) for i in range(count - 1)]
        backward = [(target, source) for source, target in forward]
        low = lax.ppermute(
            lax.slice_in_dim(block, block.shape[dim] - width, None, axis=dim), axis, forward
        )
        high = lax.ppermute(lax.slice_in_dim(block, 0, width, axis=dim), axis, backward)
        block = jnp.concatenate([low, block, high], axis=dim)
    return block


def gelu_slope(argument):
    return (
        0.5 * (1.0 + jax.scipy.special.erf(argument * 0.7071067811865476))
        + argument * jnp.exp(-0.5 * argument * argument) * 0.3989422804014327
    )


def pair_flip(matrix, strand):
    swapped = matrix.reshape(matrix.shape[0], -1, 2)[:, :, ::-1].reshape(matrix.shape)
    return jnp.where(strand[:, None] == 1, swapped, matrix)


def exon_hits(bin_lists, counts, positions):
    listed = jnp.arange(bin_lists.shape[1], dtype=jnp.int32)[None, :] < counts[:, None]
    matched = (bin_lists[:, :, None] == positions[None, None, :]) & listed[:, :, None]
    return jnp.sum(matched.astype(jnp.float32), axis=1).astype(jnp.bfloat16)


def per_device(
    features,
    norm_gain,
    convolution_taps_weight,
    out_weight,
    head_weight,
    rc_perm,
    exon_bins,
    exon_count,
    gene_strand,
    gene_target,
):
    bin_devices = lax.axis_size("bins")
    bin_index = lax.axis_index("bins")
    widened = features[0].astype(jnp.float32)
    count_of_rows = widened.shape[0]
    channels = widened.shape[1]
    inverse = lax.rsqrt(jnp.mean(widened * widened, axis=-1, keepdims=True) + 1e-06)
    normed = widened * inverse * norm_gain
    hidden_state = jax.nn.gelu(normed, approximate=False).astype(jnp.bfloat16)
    padded_input = with_halo(hidden_state, (("bins", 0),), DILATION_STEP)
    convolved_sum = jnp.zeros((count_of_rows, convolution_taps_weight.shape[2]), jnp.float32)
    for kernel_tap_index in range(3):
        convolved_sum = convolved_sum + jnp.dot(
            padded_input[
                kernel_tap_index * DILATION_STEP : kernel_tap_index * DILATION_STEP + count_of_rows
            ],
            convolution_taps_weight[kernel_tap_index],
            preferred_element_type=jnp.float32,
        )
    active = jax.nn.gelu(convolved_sum, approximate=False).astype(jnp.bfloat16)
    block_out = (widened + jnp.dot(active, out_weight, preferred_element_type=jnp.float32)).astype(
        jnp.bfloat16
    )
    part_rows = channels // bin_devices
    local_rows = lax.dynamic_slice_in_dim(head_weight, bin_index * part_rows, part_rows, 0)
    across = lax.all_gather(local_rows, "batch", axis=1, tiled=True)
    whole_head = lax.all_gather(across, "bins", axis=0, tiled=True)
    logits = jnp.dot(block_out, whole_head, preferred_element_type=jnp.float32)
    predicted = jax.nn.softplus(logits).astype(jnp.bfloat16)
    positions = bin_index * count_of_rows + jnp.arange(count_of_rows, dtype=jnp.int32)
    hit_counts = exon_hits(exon_bins[0], exon_count[0], positions)
    partial_value = jnp.dot(hit_counts, predicted, preferred_element_type=jnp.float32)
    own_genes = gene_target.shape[1]
    owned_sum = lax.psum_scatter(
        partial_value.astype(jnp.bfloat16), "bins", scatter_dimension=0, tiled=True
    ).astype(jnp.float32)
    own_strand = lax.dynamic_slice_in_dim(gene_strand[0], bin_index * own_genes, own_genes, 0)
    coverage = pair_flip(owned_sum, own_strand)
    adjoint = (1.0 - gene_target[0] / (1.0 + coverage)).astype(jnp.bfloat16)
    spread_back = lax.all_gather(pair_flip(adjoint, own_strand), "bins", axis=0, tiled=True)
    pred_grad = lax.dot_general(
        hit_counts, spread_back, (((0,), (0,)), ((), ())), preferred_element_type=jnp.float32
    )
    logit_grad = (pred_grad * jax.nn.sigmoid(logits)).astype(jnp.bfloat16)
    head_back = lax.dot_general(
        logit_grad, whole_head, (((1,), (1,)), ((), ())), preferred_element_type=jnp.float32
    )
    pieces = block_out.reshape(bin_devices, count_of_rows // bin_devices, channels)
    outbound = lax.all_to_all(pieces, "bins", split_axis=0, concat_axis=0, tiled=True)
    returned = lax.all_to_all(outbound[::-1], "bins", split_axis=0, concat_axis=0, tiled=True)
    partner = returned.reshape(count_of_rows, channels)
    mirrored = partner[::-1].astype(jnp.float32)
    inverse_perm = (
        jnp.zeros((channels,), jnp.int32).at[rc_perm].set(jnp.arange(channels, dtype=jnp.int32))
    )
    block_wide = block_out.astype(jnp.float32)
    rc_grad = block_wide - 0.5 * (mirrored[:, rc_perm] + mirrored[:, inverse_perm])
    block_grad = (head_back + rc_grad).astype(jnp.bfloat16)
    batch_share = lax.psum_scatter(
        lax.dot_general(
            active, block_grad, (((0,), (0,)), ((), ())), preferred_element_type=jnp.float32
        ).astype(jnp.bfloat16),
        "batch",
        scatter_dimension=0,
        tiled=True,
    )
    out_weight_grad = lax.psum(batch_share, "bins").astype(jnp.float32)
    activation_gradient = (
        lax.dot_general(
            block_grad, out_weight, (((1,), (1,)), ((), ())), preferred_element_type=jnp.float32
        )
        * gelu_slope(convolved_sum)
    ).astype(jnp.bfloat16)
    padded_gradient = with_halo(activation_gradient, (("bins", 0),), DILATION_STEP)
    hidden_grad = jnp.zeros((count_of_rows, channels), jnp.float32)
    for kernel_tap_index in range(3):
        shift_amount = (2 - kernel_tap_index) * DILATION_STEP
        hidden_grad = hidden_grad + lax.dot_general(
            padded_gradient[shift_amount : shift_amount + count_of_rows],
            convolution_taps_weight[kernel_tap_index],
            (((1,), (1,)), ((), ())),
            preferred_element_type=jnp.float32,
        )
    normed_grad = hidden_grad * gelu_slope(normed) * norm_gain
    norm_back = inverse * normed_grad - widened * inverse**3 * jnp.mean(
        normed_grad * widened, axis=-1, keepdims=True
    )
    input_grad = (block_grad.astype(jnp.float32) + norm_back).astype(jnp.bfloat16)
    return (input_grad[None], out_weight_grad)


def solution(mesh):
    in_specs = (
        P("batch", "bins", None),
        P(),
        P(),
        P(),
        P(None, "batch"),
        P(),
        P("batch", None, None),
        P("batch", None),
        P("batch", None),
        P("batch", "bins", None),
    )
    out_specs = (P("batch", "bins", None), P("batch", None))
    return jax.shard_map(
        per_device, mesh=mesh, in_specs=in_specs, out_specs=out_specs, check_vma=False
    )
```

profile of v0, /device:TPU:15, one launch (start us, length us, event | category | flops | bytes accessed | tf_op | source)
XLA Modules:
  0.0 372.3 jit_solution(13654827316583596669)
XLA Ops:
  9.2 62.4 %all-gather.4.cloned.1.call-done = bf16[384,4096]{1,0:T(8,128)(2,1)} async-done(((bf16[384,512]{1,0:T(8,128)(2,1)}), bf16[384,4096]{1,0:T(8,128)(2,1)}) %all-gather.4.cloned.1.call-update) | async-done | bytes 3145744 | tf_op jit(solution)/shard_map/all_gather | solution.py:76
  73.0 3.8 %fusion.39 = bf16[256,1536]{1,0:T(8,128)(2,1)S(1)} fusion(bf16[1,256,1536]{2,1,0:T(8,128)(2,1)S(1)} %copy-done.2, f32[1536]{0:T(1024)S(1)} %copy-done.10, f32[256]{0:T(256)S(1)} %get-tuple-element.7), kind=kLoop, calls=%fused_computation.54 | loop fusion | flops 26738688 | bytes 1580032 | tf_op jit(solution)/shard_map/convert_element_type | solution.py:59
  77.7 3.0 collective-permute-start.1
  82.0 6.2 %scatter_custom_fusion = s32[1536]{0:T(1024)S(1)} fusion(s32[1536]{0:T(1024)S(1)} %compare_select_fusion.2, s32[1536]{0:T(1024)S(1)} %iota.16, s32[]{:T(128)} %constant.45.clone.1), kind=kCustom, calls=%fused_computation.185 | custom fusion | bytes 6148 | tf_op jit(solution)/shard_map/scatter | solution.py:104
  88.2 7.1 %fusion.13 = f32[256,768]{1,0:T(8,128)} fusion(bf16[3,1536,768]{2,1,0:T(8,128)(2,1)} %param.12, bf16[1,256,1536]{2,1,0:T(8,128)(2,1)S(1)} %copy-done.2, f32[1536]{0:T(1024)S(1)} %copy-done.10, f32[256]{0:T(256)S(1)} %get-tuple-element.7), kind=kOutput, calls=%fused_computation.26 | convolution fusion | flops 630718464 | bytes 3939328 | tf_op jit(solution)/shard_map/dot_general | solution.py:63
  98.2 4.8 %fusion.101 = (bf16[256,768]{1,0:T(8,128)(2,1)S(1)}, f32[256,768]{1,0:T(8,128)}) fusion(f32[256,768]{1,0:T(8,128)S(1)} %fusion.9, f32[256,768]{1,0:T(8,128)S(1)} %copy-done.18, bf16[3,1536,768]{2,1,0:T(8,128)(2,1)} %param.12, bf16[256,1536]{1,0:T(8,128)(2,1)S(1)} %copy-done.6, bf16[16,1536]{1,0:T(8,128)(2,1)S(1)} %collective-permute-done), kind=kOutput, calls=%fused_computation.117 | convolution fusion | flops 618725376 | bytes 5947392 | tf_op jit(solution)/shard_map/dot_general | solution.py:63
  104.8 4.9 %all-to-all-start = ((bf16[4,64,1536]{2,1,0:T(8,128)(2,1)}), bf16[4,64,1536]{2,1,0:T(8,128)(2,1)S(1)}, u32[]{:S(2)}, u32[]{:S(2)}) async-start(bf16[4,64,1536]{2,1,0:T(8,128)(2,1)} %bitcast.188), calls=%async_computation | async-start | bytes 1572864 | tf_op jit(solution)/shard_map/all_to_all | solution.py:99
  113.1 15.6 %all-to-all-done = bf16[4,64,1536]{2,1,0:T(8,128)(2,1)S(1)} async-done(((bf16[4,64,1536]{2,1,0:T(8,128)(2,1)}), bf16[4,64,1536]{2,1,0:T(8,128)(2,1)S(1)}, u32[]{:S(2)}, u32[]{:S(2)}) %all-to-all-start) | async-done | bytes 786464 | tf_op jit(solution)/shard_map/all_to_all | solution.py:99
  129.7 4.8 %all-to-all-start.1 = ((bf16[4,64,1536]{2,1,0:T(8,128)(2,1)}), bf16[4,64,1536]{2,1,0:T(8,128)(2,1)S(1)}, u32[]{:S(2)}, u32[]{:S(2)}) async-start(bf16[4,64,1536]{2,1,0:T(8,128)(2,1)} %rev.14), calls=%async_computation.1 | async-start | bytes 1572864 | tf_op jit(solution)/shard_map/all_to_all | solution.py:100
  134.5 38.5 %all-gather.6.cloned.1.call-done = bf16[1536,4096]{1,0:T(8,128)(2,1)} async-done(((bf16[384,4096]{1,0:T(8,128)(2,1)}), bf16[1536,4096]{1,0:T(8,128)(2,1)}) %all-gather.6.cloned.1.call-update) | async-done | bytes 12582928 | tf_op jit(solution)/shard_map/all_gather | solution.py:77
  173.1 6.6 %fusion.195 = f32[256,4096]{1,0:T(8,128)S(1)} fusion(bf16[256,1536]{1,0:T(8,128)(2,1)} %fusion.6, bf16[1536,4096]{1,0:T(8,128)(2,1)} %all-gather.6.cloned.1.call-done), kind=kOutput, calls=%fused_computation.234 | convolution fusion | flops 3221225472 | bytes 17563648 | tf_op jit(solution)/shard_map/dot_general | solution.py:78
  186.0 10.3 %rev.15 = bf16[256,1536]{0,1:T(8,128)(2,1)S(1)} reverse(bf16[256,1536]{0,1:T(8,128)(2,1)} %copy.35), dimensions={0} | reverse | bytes 1572864 | tf_op jit(solution)/shard_map/rev | solution.py:102
  197.6 6.1 %gather_fusion.1 = f32[1536,256]{1,0:T(8,128)} fusion(f32[256,1536]{0,1:T(8,128)} %convert_element_type.84, s32[2048]{0:T(1024)S(1)} %pad_clamp_fusion), kind=kCustom, calls=%fused_computation.1 | custom fusion | bytes 3151872 | tf_op jit(solution)/shard_map/gather | solution.py:107
  206.7 6.1 %gather_fusion = f32[1536,256]{1,0:T(8,128)} fusion(f32[256,1536]{0,1:T(8,128)} %convert_element_type.84, s32[2048]{0:T(1024)S(1)} %pad_clamp_fusion.1), kind=kCustom, calls=%fused_computation | custom fusion | bytes 3151872 | tf_op jit(solution)/shard_map/gather | solution.py:107
  212.8 3.0 copy.36
  217.2 7.8 %rev.12 = f32[4,2048,2]{0,2,1:T(2,128)} reverse(bf16[4,2048,2]{0,2,1:T(2,128)(2,1)S(1)} %bitcast.183), dimensions={2} | reverse | bytes 98304 | tf_op jit(solution)/shard_map/rev | solution.py:30
  225.1 3.7 fusion.19
  228.8 10.3 %rev.13 = bf16[4,2048,2]{0,2,1:T(2,128)(2,1)} reverse(bf16[4,2048,2]{0,2,1:T(2,128)(2,1)} %bitcast.184), dimensions={2} | reverse | bytes 65536 | tf_op jit(solution)/shard_map/rev | solution.py:30
  242.9 6.2 %all-gather = bf16[4,4,4096]{2,1,0:T(4,128)(2,1)S(1)} all-gather(bf16[1,4,4096]{2,1,0:T(4,128)(2,1)S(1)} %copy.34), channel_id=1, replica_groups=mesh['bins'=4,'batch'=8] {'bins'}, dimensions={0}, use_global_device_ids=true | all-gather | bytes 163840 | tf_op jit(solution)/shard_map/all_gather | solution.py:90
  249.8 9.9 %fusion.5 = bf16[256,1536]{1,0:T(8,128)(2,1)S(1)} fusion(bf16[1536,4096]{1,0:T(8,128)(2,1)} %all-gather.6.cloned.1.call-done, bf16[16,4096]{1,0:T(8,128)(2,1)} %reshape.131, f32[256,4096]{1,0:T(8,128)} %copy-done.17, f32[1536,256]{0,1:T(8,128)} %copy.36, f32[1536,256]{0,1:T(8,128)} %copy.37, bf16[256,1536]{1,0:T(8,128)(2,1)} %fusion.6, ...), kind=kOutput, calls=%fused_computation.15 | convolution fusion | flops 3262382080 | bytes 21635072 | tf_op jit(solution)/shard_map/dot_general | solution.py:95
  267.9 3.2 collective-permute-start.2
  273.6 4.2 %fusion.56 = (f32[256]{0:T(256)S(1)}, f32[256,1536]{1,0:T(8,128)}) fusion(bf16[1,256,1536]{2,1,0:T(8,128)(2,1)S(1)} %copy-done.3, f32[1536]{0:T(1024)S(1)} %copy-done.10, f32[256]{0:T(256)S(1)} %get-tuple-element.7, f32[256,1536]{1,0:T(8,128)S(1)} %fusion.7, f32[256,1536]{1,0:T(8,128)S(1)} %fusion.11, bf16[3,1536,768]{2,1,0:T(8,128)(2,1)} %param.12, ...), kind=kOutput, calls=%fused_computation.71 | convolution fusion | flops 611450624 | bytes 8290304 | tf_op jit(solution)/shard_map/dot_general | solution.py:128
  277.8 51.4 %reduce-scatter.2.cloned.1.call-done = bf16[96,1536]{1,0:T(8,128)(2,1)} async-done(((bf16[768,1536]{1,0:T(8,128)(2,1)}), bf16[96,1536]{1,0:T(8,128)(2,1)}) %reduce-scatter.2.cloned.1.call-update) | async-done | bytes 294928 | tf_op jit(solution)/shard_map/reduce_scatter | solution.py:109
  332.1 31.8 %all-reduce.4.cloned.1.call-done = bf16[96,1536]{1,0:T(8,128)(2,1)} async-done(((bf16[96,1536]{1,0:T(8,128)(2,1)}), bf16[96,1536]{1,0:T(8,128)(2,1)}) %all-reduce.4.cloned.1.call-update) | async-done | bytes 294928 | tf_op jit(solution)/shard_map/psum | solution.py:117
  (92 shorter events, 45.9 us)
Async XLA Ops:
  7.2 95.9 %copy-start = (bf16[768,1536]{1,0:T(8,128)(2,1)S(1)}, bf16[768,1536]{1,0:T(8,128)(2,1)}, u32[]{:S(2)}) copy-start(bf16[768,1536]{1,0:T(8,128)(2,1)} %param.13) | copy-start | bytes 7077892
  7.2 64.4 %all-gather.4.cloned.1.call-start = ((), (), s32[]{:S(2)}) async-start(), calls=%async_computation.3 | async-start | bytes 3538944 | tf_op jit(solution)/shard_map/all_gather | solution.py:76
  9.2 163.9 %all-gather.6.cloned.1.call-start = ((), (), s32[]{:S(2)}) async-start(), calls=%async_computation.4 | async-start | bytes 15728640 | tf_op jit(solution)/shard_map/all_gather | solution.py:77
  72.8 9.3 %copy-start.11 = (s32[1536]{0:T(1024)S(1)}, s32[1536]{0:T(1024)}, u32[]{:S(2)}) copy-start(s32[1536]{0:T(1024)} %param.15) | copy-start | bytes 18436
  77.7 17.6 %collective-permute-start.1 = (bf16[16,1536]{1,0:T(8,128)(2,1)S(1)}, bf16[16,1536]{1,0:T(8,128)(2,1)S(1)}, u32[]{:S(2)}, u32[]{:S(2)}) collective-permute-start(bf16[16,1536]{1,0:T(8,128)(2,1)S(1)} %get-tuple-element.3), channel_id=1, source_target_pairs={{8,0},{16,8},{24,16},{9,1},{17,9},{25,17},{10,2},{18,10},{26,18},{... | collective-permute-start | bytes 147464 | tf_op jit(solution)/shard_map/ppermute | solution.py:17
  80.7 17.5 %collective-permute-start = (bf16[16,1536]{1,0:T(8,128)(2,1)S(1)}, bf16[16,1536]{1,0:T(8,128)(2,1)S(1)}, u32[]{:S(2)}, u32[]{:S(2)}) collective-permute-start(bf16[16,1536]{1,0:T(8,128)(2,1)S(1)} %get-tuple-element.2), channel_id=1, source_target_pairs={{0,8},{8,16},{16,24},{1,9},{9,17},{17,25},{2,10},{10,18},{18,26},{... | collective-permute-start | bytes 147464 | tf_op jit(solution)/shard_map/ppermute | solution.py:14
  95.3 2.9 copy-start.6
  95.3 2.9 copy-start.18
  104.8 4.9 %copy-start.13 = (s32[1,16,8]{1,2,0:T(8,128)S(1)}, s32[1,16,8]{1,2,0:T(8,128)}, u32[]{:S(2)}) copy-start(s32[1,16,8]{1,2,0:T(8,128)} %param.16) | copy-start | bytes 1540
  104.8 5.0 %copy-start.9 = (f32[1,4,4096]{2,1,0:T(4,128)S(1)}, f32[1,4,4096]{2,1,0:T(4,128)}, u32[]{:S(2)}) copy-start(f32[1,4,4096]{2,1,0:T(4,128)} %param.19) | copy-start | bytes 196612
  104.8 6.9 %copy-start.16 = (u32[32]{0:T(128)S(1)}, u32[32]{0:T(128)}, u32[]{:S(2)}) copy-start(u32[32]{0:T(128)} %constant.16) | copy-start | bytes 388
  104.8 8.1 %copy-start.14 = (s32[1,16]{1,0:T(1,128)S(1)}, s32[1,16]{1,0:T(1,128)}, u32[]{:S(2)}) copy-start(s32[1,16]{1,0:T(1,128)} %param.17) | copy-start | bytes 196
  104.8 23.9 %all-to-all-start = ((bf16[4,64,1536]{2,1,0:T(8,128)(2,1)}), bf16[4,64,1536]{2,1,0:T(8,128)(2,1)S(1)}, u32[]{:S(2)}, u32[]{:S(2)}) async-start(bf16[4,64,1536]{2,1,0:T(8,128)(2,1)} %bitcast.188), calls=%async_computation | async-start | bytes 1572864 | tf_op jit(solution)/shard_map/all_to_all | solution.py:99
  113.1 66.6 %copy-start.12 = (bf16[16,256]{1,0:T(8,128)(2,1)}, bf16[16,256]{1,0:T(8,128)(2,1)S(1)}, u32[]{:S(2)}) copy-start(bf16[16,256]{1,0:T(8,128)(2,1)S(1)} %convert_reduce_fusion) | copy-start | bytes 24580
  129.7 55.2 %all-to-all-start.1 = ((bf16[4,64,1536]{2,1,0:T(8,128)(2,1)}), bf16[4,64,1536]{2,1,0:T(8,128)(2,1)S(1)}, u32[]{:S(2)}, u32[]{:S(2)}) async-start(bf16[4,64,1536]{2,1,0:T(8,128)(2,1)} %rev.14), calls=%async_computation.1 | async-start | bytes 1572864 | tf_op jit(solution)/shard_map/all_to_all | solution.py:100
  134.5 81.4 %all-reduce.6.cloned.1.call-start = ((), (), s32[]{:S(2)}) async-start(), calls=%async_computation.7 | async-start | bytes 262144
  181.7 3.1 copy-start.15
  184.7 144.5 %reduce-scatter.2.cloned.1.call-start = ((), (), s32[]{:S(2)}) async-start(), calls=%async_computation.5 | async-start | bytes 2654208 | tf_op jit(solution)/shard_map/reduce_scatter | solution.py:109
  228.8 10.3 %copy-start.1 = (bf16[4,4096]{0,1:T(8,128)(2,1)S(1)}, bf16[4,4096]{0,1:T(8,128)(2,1)}, u32[]{:S(2)}) copy-start(bf16[4,4096]{0,1:T(8,128)(2,1)} %fusion.19) | copy-start | bytes 98308
  249.8 9.9 %copy-start.8 = (bf16[256,768]{1,0:T(8,128)(2,1)S(1)}, bf16[256,768]{1,0:T(8,128)(2,1)}, u32[]{:S(2)}) copy-start(bf16[256,768]{1,0:T(8,128)(2,1)} %copy-done.7) | copy-start | bytes 1179652
  262.0 102.0 %all-reduce.4.cloned.1.call-start = ((), (), s32[]{:S(2)}) async-start(), calls=%async_computation.6 | async-start | bytes 589824 | tf_op jit(solution)/shard_map/psum | solution.py:117
  264.1 7.0 %collective-permute-start.3 = (bf16[16,768]{1,0:T(8,128)(2,1)S(1)}, bf16[16,768]{1,0:T(8,128)(2,1)S(1)}, u32[]{:S(2)}, u32[]{:S(2)}) collective-permute-start(bf16[16,768]{1,0:T(8,128)(2,1)S(1)} %get-tuple-element.5), channel_id=1, source_target_pairs={{0,8},{8,16},{16,24},{1,9},{9,17},{17,25},{2,10},{10,18},{18,26},{... | collective-permute-start | bytes 73736 | tf_op jit(solution)/shard_map/ppermute | solution.py:14
  267.9 5.7 %copy-start.3 = (bf16[1,256,1536]{2,1,0:T(8,128)(2,1)S(1)}, bf16[1,256,1536]{2,1,0:T(8,128)(2,1)}, u32[]{:S(2)}) copy-start(bf16[1,256,1536]{2,1,0:T(8,128)(2,1)} %param.10) | copy-start | bytes 2359300
  267.9 5.7 %collective-permute-start.2 = (bf16[16,768]{1,0:T(8,128)(2,1)S(1)}, bf16[16,768]{1,0:T(8,128)(2,1)S(1)}, u32[]{:S(2)}, u32[]{:S(2)}) collective-permute-start(bf16[16,768]{1,0:T(8,128)(2,1)S(1)} %get-tuple-element.4), channel_id=1, source_target_pairs={{8,0},{16,8},{24,16},{9,1},{17,9},{25,17},{10,2},{18,10},{26,18},{... | collective-permute-start | bytes 73736 | tf_op jit(solution)/shard_map/ppermute | solution.py:17
  (6 other events, 9.4 us)
Sparse Core Ops, SparseCore 0:
  10.6 60.9 all-gather.3
  73.2 99.8 all-gather.5
  184.8 30.3 all-reduce.5
  262.1 66.9 reduce-scatter.1
  331.5 32.4 all-reduce.3
where the time goes:
time: 378 us; the launch traced here: 372 us
  waiting for transfers between devices  200 us (53%)
  local copies, waits for them, and re-layouts  67.1 us (18%)
  matrix products  49.5 us (13%)
  starting transfers between devices  18.6 us (5%)
  other arithmetic  16.4 us (4%)
  between operations  14.7 us (4%)
  blocking collectives  6.18 us (2%)
    all_gather x1, waiting for transfers between devices, per_device(): across = lax.all_gather(local_rows, 'batch', axis=1, tiled=True)  62.4 us
    reduce_scatter x1, waiting for transfers between devices, per_device(): lax.psum_scatter(lax.dot_general(active, block_grad, (((0,), (0,)), ((),...  51.4 us
    all_gather x1, waiting for transfers between devices, per_device(): whole_head = lax.all_gather(across, 'bins', axis=0, tiled=True)  38.5 us
    psum x1, waiting for transfers between devices, per_device(): out_weight_grad = lax.psum(batch_share, 'bins').astype(jnp.float32)  31.8 us
    rev x2, local copies, waits for them, and re-layouts, pair_flip(): matrix.reshape(matrix.shape[0], -1, 2)[:, :, ::-1].reshape(matrix.shape)  18.1 us
    all_to_all x1, waiting for transfers between devices, per_device(): lax.all_to_all(pieces, 'bins', split_axis=0, concat_axis=0, tiled=True)  15.6 us
    dot_general x3, matrix products, per_device(): jnp.dot(padded_input[kernel_tap_index * DILATION_STEP:kernel_tap_index *...  14.8 us
    rev x1, local copies, waits for them, and re-layouts, per_device(): mirrored = partner[::-1].astype(jnp.float32)  10.3 us
  transfers between devices with their start and end apart: 11, of which 5 were waited for; matrix products, arithmetic and copies ran while one was open for 23% of the time, Pallas kernels for 0%

commit v1 on v0

v1 whole, which is shorter than its diff:
```python
import functools

import jax
import jax.numpy as jnp
from jax import lax
from jax.experimental import pallas as pl
from jax.experimental.pallas import tpu as pltpu
from jax.sharding import PartitionSpec as P

DILATION_STEP = 16
MESH = pl.DeviceIdType.MESH
BF = jnp.bfloat16
F32 = jnp.float32


def greet(axis, count):
    me = lax.axis_index(axis)
    barrier = pltpu.get_barrier_semaphore()
    for step in range(1, count):
        pl.semaphore_signal(
            barrier,
            inc=1,
            device_id={axis: lax.rem(me + step, count)},
            device_id_type=MESH,
        )
    pl.semaphore_wait(barrier, count - 1)
    return me


def exchange_kernel(axis, count, x_ref, o_ref, local, send_sem, recv_sem):
    me = greet(axis, count)
    copies = []
    for step in range(1, count):
        peer = lax.rem(me + step, count)
        copy = pltpu.make_async_remote_copy(
            src_ref=x_ref.at[peer],
            dst_ref=o_ref.at[me],
            send_sem=send_sem.at[step],
            recv_sem=recv_sem.at[step],
            device_id={axis: peer},
            device_id_type=MESH,
        )
        copy.start()
        copies.append(copy)
    mine = pltpu.make_async_copy(x_ref.at[me], o_ref.at[me], local)
    mine.start()
    mine.wait()
    for copy in copies:
        copy.wait()


def gather_kernel(axis, count, x_ref, o_ref, local, send_sem, recv_sem):
    me = greet(axis, count)
    copies = []
    for step in range(1, count):
        peer = lax.rem(me + step, count)
        copy = pltpu.make_async_remote_copy(
            src_ref=x_ref,
            dst_ref=o_ref.at[me],
            send_sem=send_sem.at[step],
            recv_sem=recv_sem.at[step],
            device_id={axis: peer},
            device_id_type=MESH,
        )
        copy.start()
        copies.append(copy)
    mine = pltpu.make_async_copy(x_ref, o_ref.at[me], local)
    mine.start()
    mine.wait()
    for copy in copies:
        copy.wait()


def reduce_kernel(axis, count, x_ref, o_ref, held, send_sem, recv_sem):
    me = greet(axis, count)
    copies = []
    for step in range(1, count):
        peer = lax.rem(me + step, count)
        copy = pltpu.make_async_remote_copy(
            src_ref=x_ref.at[peer],
            dst_ref=held.at[step],
            send_sem=send_sem.at[step],
            recv_sem=recv_sem.at[step],
            device_id={axis: peer},
            device_id_type=MESH,
        )
        copy.start()
        copies.append(copy)
    total = x_ref[me].astype(F32)
    for step in range(1, count):
        copies[step - 1].wait_recv()
        total = total + held[step].astype(F32)
    o_ref[...] = total.astype(o_ref.dtype)
    for copy in copies:
        copy.wait_send()


def vmem():
    return pl.BlockSpec(memory_space=pltpu.VMEM)


def run(kernel, x, out, scratch, collective_id, count):
    return pl.pallas_call(
        kernel,
        out_shape=out,
        in_specs=[vmem()],
        out_specs=vmem(),
        scratch_shapes=[
            scratch,
            pltpu.SemaphoreType.DMA((count,)),
            pltpu.SemaphoreType.DMA((count,)),
        ],
        compiler_params=pltpu.CompilerParams(
            collective_id=collective_id,
            has_side_effects=True,
            vmem_limit_bytes=32 * 1024 * 1024,
        ),
    )(x)


def exchange(x, axis, cid):
    count = lax.axis_size(axis)
    return run(
        functools.partial(exchange_kernel, axis, count),
        x,
        jax.ShapeDtypeStruct(x.shape, x.dtype),
        pltpu.SemaphoreType.DMA,
        cid,
        count,
    )


def gather(x, axis, cid):
    count = lax.axis_size(axis)
    return run(
        functools.partial(gather_kernel, axis, count),
        x,
        jax.ShapeDtypeStruct((count,) + x.shape, x.dtype),
        pltpu.SemaphoreType.DMA,
        cid,
        count,
    )


def reduce_pieces(x, axis, cid):
    count = lax.axis_size(axis)
    return run(
        functools.partial(reduce_kernel, axis, count),
        x,
        jax.ShapeDtypeStruct(x.shape[1:], x.dtype),
        pltpu.VMEM(x.shape, x.dtype),
        cid,
        count,
    )


def with_halo(block, axis, width):
    count = lax.axis_size(axis)
    forward = [(i, i + 1) for i in range(count - 1)]
    backward = [(target, source) for source, target in forward]
    low = lax.ppermute(block[-width:], axis, forward)
    high = lax.ppermute(block[:width], axis, backward)
    return jnp.concatenate([low, block, high], axis=0)


def gelu_slope(argument):
    return (
        0.5 * (1.0 + jax.scipy.special.erf(argument * 0.7071067811865476))
        + argument * jnp.exp(-0.5 * argument * argument) * 0.3989422804014327
    )


def dot(a, b, dims=((1,), (0,))):
    return lax.dot_general(a, b, (dims, ((), ())), preferred_element_type=F32)


def per_device(
    features,
    norm_gain,
    taps,
    out_weight,
    head_weight,
    rc_perm,
    exon_bins,
    exon_count,
    gene_strand,
    gene_target,
):
    bin_devices = lax.axis_size("bins")
    batch_devices = lax.axis_size("batch")
    bin_index = lax.axis_index("bins")
    rows, channels = features.shape[1:]
    hid = taps.shape[2]
    genes, exons = exon_bins.shape[1:]
    own_genes = gene_target.shape[1]
    tracks = gene_target.shape[2]
    part = head_weight.shape[1]
    own_rows = own_genes * exons

    own_strand = lax.dynamic_slice_in_dim(gene_strand[0], bin_index * own_genes, own_genes, 0)
    own_count = lax.dynamic_slice_in_dim(exon_count[0], bin_index * own_genes, own_genes, 0)
    target = gene_target[0]
    lane = lax.broadcasted_iota(jnp.int32, target.shape, 1)
    swapped = jnp.where(lane % 2 == 0, jnp.roll(target, -1, axis=1), jnp.roll(target, 1, axis=1))
    target = jnp.where(own_strand[:, None] == 1, swapped, target)
    pieces = target.reshape(own_genes, batch_devices, part).transpose(1, 0, 2)
    counted = jnp.broadcast_to(
        own_count.astype(F32)[None, :, None], (batch_devices, own_genes, 128)
    )
    arrived = exchange(jnp.concatenate([pieces, counted], axis=2), "batch", 1)
    track_target = arrived[:, :, :part]
    track_count = arrived[:, :, part : part + 1].astype(jnp.int32)

    widened = features[0].astype(F32)
    inverse = lax.rsqrt(jnp.mean(widened * widened, axis=-1, keepdims=True) + 1e-06)
    normed = widened * inverse * norm_gain
    hidden = jax.nn.gelu(normed, approximate=False).astype(BF)
    padded = with_halo(hidden, "bins", DILATION_STEP)
    conv_sum = jnp.zeros((rows, hid), F32)
    for tap in range(3):
        conv_sum = conv_sum + dot(
            padded[tap * DILATION_STEP : tap * DILATION_STEP + rows], taps[tap]
        )
    active = jax.nn.gelu(conv_sum, approximate=False).astype(BF)
    block_out = (widened + dot(active, out_weight)).astype(BF)

    partner = lax.ppermute(
        block_out, "bins", [(i, bin_devices - 1 - i) for i in range(bin_devices)]
    )

    positions = bin_index * rows + jnp.arange(rows, dtype=jnp.int32)
    listed = jnp.arange(exons, dtype=jnp.int32)[None, :] < exon_count[0][:, None]
    hits = (
        (exon_bins[0][:, :, None] == positions[None, None, :]) & listed[:, :, None]
    ).reshape(genes * exons, rows).astype(BF)
    picked = dot(hits, block_out).astype(BF).reshape(bin_devices, own_rows, channels)
    own_picked = reduce_pieces(picked, "bins", 2)
    all_picked = gather(own_picked, "batch", 3).reshape(batch_devices * own_rows, channels)

    logits = dot(all_picked, head_weight).reshape(batch_devices, own_genes, exons, part)
    predicted = jax.nn.softplus(logits).astype(BF).astype(F32)
    counts = lax.broadcasted_iota(jnp.int32, (1, 1, exons, 1), 2) < track_count[..., None]
    partial = jnp.sum(jnp.where(counts, predicted, 0.0), axis=2)
    spread = (1.0 - track_target / (1.0 + partial)).astype(BF).astype(F32)
    logit_grad = jnp.where(counts, spread[:, :, None, :] * jax.nn.sigmoid(logits), 0.0).astype(BF)
    picked_grad = dot(
        logit_grad.reshape(batch_devices * own_rows, part), head_weight, ((1,), (1,))
    ).astype(BF).reshape(batch_devices, own_rows, channels)
    own_grad = reduce_pieces(picked_grad, "batch", 4)
    seq_grad = gather(own_grad, "bins", 5).reshape(genes * exons, channels)
    head_back = dot(hits, seq_grad, ((0,), (0,)))

    flip = (
        lax.broadcasted_iota(jnp.int32, (rows, rows), 0)
        == rows - 1 - lax.broadcasted_iota(jnp.int32, (rows, rows), 1)
    ).astype(BF)
    down = lax.broadcasted_iota(jnp.int32, (channels, channels), 0)
    along = lax.broadcasted_iota(jnp.int32, (channels, channels), 1)
    both_maps = (
        (down == rc_perm[None, :]).astype(F32) + (rc_perm[:, None] == along).astype(F32)
    ).astype(BF)
    mirrored = dot(flip, partner).astype(BF)
    rc_grad = block_out.astype(F32) - 0.5 * dot(mirrored, both_maps)
    block_grad = (head_back + rc_grad).astype(BF)

    act_grad = (dot(block_grad, out_weight, ((1,), (1,))) * gelu_slope(conv_sum)).astype(BF)
    padded_grad = with_halo(act_grad, "bins", DILATION_STEP)

    weight_terms = dot(active, block_grad, ((0,), (0,))).astype(BF)
    wide = channels // bin_devices
    weight_terms = weight_terms.reshape(hid, bin_devices, wide).transpose(1, 0, 2)
    bins_sum = reduce_pieces(weight_terms, "bins", 6)
    own_sum = reduce_pieces(
        bins_sum.reshape(batch_devices, hid // batch_devices, wide), "batch", 7
    )
    out_weight_grad = gather(own_sum, "bins", 8).transpose(1, 0, 2)
    out_weight_grad = out_weight_grad.reshape(hid // batch_devices, channels).astype(F32)

    hidden_grad = jnp.zeros((rows, channels), F32)
    for tap in range(3):
        shift = (2 - tap) * DILATION_STEP
        hidden_grad = hidden_grad + dot(
            padded_grad[shift : shift + rows], taps[tap], ((1,), (1,))
        )
    normed_grad = hidden_grad * gelu_slope(normed) * norm_gain
    norm_back = inverse * normed_grad - widened * inverse**3 * jnp.mean(
        normed_grad * widened, axis=-1, keepdims=True
    )
    input_grad = (block_grad.astype(F32) + norm_back).astype(BF)
    return (input_grad[None], out_weight_grad)


def solution(mesh):
    in_specs = (
        P("batch", "bins", None),
        P(),
        P(),
        P(),
        P(None, "batch"),
        P(),
        P("batch", None, None),
        P("batch", None),
        P("batch", None),
        P("batch", "bins", None),
    )
    out_specs = (P("batch", "bins", None), P("batch", None))
    return jax.shard_map(
        per_device, mesh=mesh, in_specs=in_specs, out_specs=out_specs, check_vma=False
    )
```

time: 378 us -> 202 us (0.53); the launches traced: 372 us -> 202 us
  waiting for transfers between devices: 200 us -> 0.01 us
  Pallas kernels: 0 us -> 132 us
  local copies, waits for them, and re-layouts: 67.1 us -> 12.7 us
  between operations: 14.7 us -> 1.19 us
  matrix products: 49.5 us -> 36.7 us
  starting transfers between devices: 18.6 us -> 8.65 us
  other arithmetic: 16.4 us -> 10.1 us
  blocking collectives: 6.18 us -> 0 us
    pallas_call x0 -> x8, Pallas kernels: none -> 132 us  [run(): pl.pallas_call(kernel, out_shape=out, in_specs=[vmem()], out_specs=vmem()...]
    all_gather x2 -> x0, waiting for transfers between devices: 101 us -> none  [the longest x1 62.4 us: per_device(): across = lax.all_gather(local_rows, 'batch', axis=1, tiled=True)]
    reduce_scatter x1 -> x0, waiting for transfers between devices: 51.4 us -> none  [per_device(): lax.psum_scatter(lax.dot_general(active, block_grad, (((0,), (0,)), ((),...]
    psum x1 -> x0, waiting for transfers between devices: 31.8 us -> none  [per_device(): out_weight_grad = lax.psum(batch_share, 'bins').astype(jnp.float32)]
    rev x4 -> x0, local copies, waits for them, and re-layouts: 29.4 us -> none  [the longest x2 18.1 us: pair_flip(): matrix.reshape(matrix.shape[0], -1, 2)[:, :, ::-1].reshape(matrix.shape)]
    gather x4 -> x0, local copies, waits for them, and re-layouts: 18.2 us -> none  [the longest x2 9.12 us: per_device(): mirrored[:, rc_perm] + mirrored[:, inverse_perm]]
    all_to_all x2 -> x0, waiting for transfers between devices: 15.6 us -> none  [the longest x1 15.6 us: per_device(): lax.all_to_all(pieces, 'bins', split_axis=0, concat_axis=0, tiled=True)]
    dot_general x12 -> x14, matrix products: 49.5 us -> 36.7 us  [dot(): return lax.dot_general(a, b, (dims, ((), ())), preferred_element_type=F32)]
  transfers between devices with their start and end apart: 11 -> 5, of which waited for: 5 -> 0; matrix products, arithmetic and copies ran while one was open for 23% -> 13% of each run, Pallas kernels for 0% -> 66%
where the time goes in v1:
time: 202 us
  Pallas kernels  132 us (65%)
  matrix products  36.7 us (18%)
  local copies, waits for them, and re-layouts  12.7 us (6%)
  other arithmetic  10.1 us (5%)
  starting transfers between devices  8.65 us (4%)
    pallas_call x8, Pallas kernels, run(): pl.pallas_call(kernel, out_shape=out, in_specs=[vmem()], out_specs=vmem()...  132 us
    dot_general x14, matrix products, dot(): return lax.dot_general(a, b, (dims, ((), ())), preferred_element_type=F32)  36.7 us
    ppermute x2, starting transfers between devices, with_halo(): high = lax.ppermute(block[:width], axis, backward)  5.1 us
    convert_element_type x1, other arithmetic, per_device(): hidden = jax.nn.gelu(normed, approximate=False).astype(BF)  4.77 us
    convert_element_type x1, local copies, waits for them, and re-layouts, per_device(): weight_terms = dot(active, block_grad, ((0,), (0,))).astype(BF)  4.29 us
    reshape x1, local copies, waits for them, and re-layouts, per_device(): weight_terms.reshape(hid, bin_devices, wide).transpose(1, 0, 2)  4.25 us
  transfers between devices with their start and end apart: 5, of which 0 were waited for; matrix products, arithmetic and copies ran while one was open for 13% of the time, Pallas kernels for 66%

profile of v1, /device:TPU:15, one launch (start us, length us, event | category | flops | bytes accessed | tf_op | source)
XLA Modules:
  0.0 201.7 jit_solution(15365648480019747544)
XLA Ops:
  0.7 1.5 fusion.31
  2.8 4.8 %fusion.38 = bf16[256,1536]{1,0:T(8,128)(2,1)S(1)} fusion(bf16[1,256,1536]{2,1,0:T(8,128)(2,1)} %param.10, f32[1536]{0:T(1024)} %param.11, f32[256]{0:T(256)S(1)} %get-tuple-element.11), kind=kLoop, calls=%fused_computation.53 | loop fusion | flops 26738688 | bytes 1580032 | tf_op jit(solution)/shard_map/convert_element_type | solution.py:217
  9.8 3.8 %collective-permute-start.1 = (bf16[16,1536]{1,0:T(8,128)(2,1)S(1)}, bf16[16,1536]{1,0:T(8,128)(2,1)}, u32[]{:S(2)}, u32[]{:S(2)}) collective-permute-start(bf16[16,1536]{1,0:T(8,128)(2,1)S(1)} %get-tuple-element.3), channel_id=1, source_target_pairs={{8,0},{16,8},{24,16},{9,1},{17,9},{25,17},{10,2},{18,10},{26,18},{... | collective-permute-start | bytes 147464 | tf_op jit(solution)/shard_map/ppermute | solution.py:162
  14.9 5.8 %shard_map.113 = f32[8,4,640]{2,1,0:T(4,128)S(1)} custom-call(f32[8,4,640]{2,1,0:T(4,128)S(1)} %pad_maximum_fusion.8.x_ref), custom_call_target="tpu_custom_call" | custom-call | tf_op jit(solution)/shard_map/pallas_call | solution.py:103
  21.0 6.8 %fusion.16 = f32[256,768]{1,0:T(8,128)} fusion(bf16[3,1536,768]{2,1,0:T(8,128)(2,1)} %param.12, bf16[1,256,1536]{2,1,0:T(8,128)(2,1)S(1)} %copy-done.2, f32[1536]{0:T(1024)S(1)} %copy-done.12, f32[256]{0:T(256)S(1)} %get-tuple-element.11), kind=kOutput, calls=%fused_computation.29 | convolution fusion | flops 630718464 | bytes 3939328 | tf_op jit(solution)/shard_map/dot_general | solution.py:174
  28.1 2.8 %fusion.12 = f32[256,768]{1,0:T(8,128)S(1)} fusion(bf16[3,1536,768]{2,1,0:T(8,128)(2,1)} %param.12, bf16[16,1536]{1,0:T(8,128)(2,1)} %collective-permute-done.1, bf16[256,1536]{1,0:T(8,128)(2,1)} %copy-done.5), kind=kOutput, calls=%fused_computation.25 | convolution fusion | flops 605552640 | bytes 3981312 | tf_op jit(solution)/shard_map/dot_general | solution.py:174
  30.9 4.9 %fusion.102 = (bf16[256,768]{1,0:T(8,128)(2,1)S(1)}, f32[256,768]{1,0:T(8,128)}) fusion(f32[256,768]{1,0:T(8,128)S(1)} %fusion.12, f32[256,768]{1,0:T(8,128)S(1)} %copy-done.23, bf16[3,1536,768]{2,1,0:T(8,128)(2,1)} %param.12, bf16[256,1536]{1,0:T(8,128)(2,1)S(1)} %copy-done.6, bf16[16,1536]{1,0:T(8,128)(2,1)} %collective-permute-done), kind=kOutput, calls=%fused_computation.116 | convolution fusion | flops 618725376 | bytes 5947392 | tf_op jit(solution)/shard_map/dot_general | solution.py:174
  37.9 22.9 %shard_map.114.x_ref = bf16[32,1536]{1,0:T(8,128)(2,1)S(1)} custom-call(bf16[4,32,1536]{2,1,0:T(8,128)(2,1)S(1)} %bitcast.197), custom_call_target="tpu_custom_call" | custom-call | tf_op jit(solution)/shard_map/pallas_call | solution.py:103
  60.8 22.0 %shard_map.115 = bf16[8,32,1536]{2,1,0:T(8,128)(2,1)S(1)} custom-call(bf16[32,1536]{1,0:T(8,128)(2,1)S(1)} %shard_map.114.x_ref), custom_call_target="tpu_custom_call" | custom-call | tf_op jit(solution)/shard_map/pallas_call | solution.py:103
  84.7 21.4 %shard_map.116.x_ref = bf16[32,1536]{1,0:T(8,128)(2,1)S(1)} custom-call(bf16[8,32,1536]{2,1,0:T(8,128)(2,1)S(1)} %bitcast.194), custom_call_target="tpu_custom_call" | custom-call | tf_op jit(solution)/shard_map/pallas_call | solution.py:103
  106.2 7.2 %shard_map.117 = bf16[4,32,1536]{2,1,0:T(8,128)(2,1)S(1)} custom-call(bf16[32,1536]{1,0:T(8,128)(2,1)S(1)} %shard_map.116.x_ref), custom_call_target="tpu_custom_call" | custom-call | tf_op jit(solution)/shard_map/pallas_call | solution.py:103
  113.4 5.3 %fusion.7 = f32[256,1536]{1,0:T(8,128)} fusion(s32[1536]{0:T(1024)} %param.15, bf16[256,1536]{1,0:T(8,128)(2,1)S(1)} %copy-done.8, bf16[256,1536]{1,0:T(8,128)(2,1)} %collective-permute-done.2, s32[256]{0:T(256)} %iota_subtract_fusion), kind=kOutput, calls=%fused_computation.14 | convolution fusion | flops 1425080320 | bytes 3152896 | tf_op jit(solution)/shard_map/dot_general | solution.py:174
  118.7 2.0 fusion.9
  121.6 3.8 %fusion.14 = f32[256,1536]{1,0:T(8,128)} fusion(bf16[256,768]{1,0:T(8,128)(2,1)S(1)} %fusion.99, bf16[3,1536,768]{2,1,0:T(8,128)(2,1)} %param.12), kind=kOutput, calls=%fused_computation.27 | convolution fusion | flops 603979776 | bytes 4325376 | tf_op jit(solution)/shard_map/dot_general | solution.py:174
  125.5 2.2 %convolution_convert_fusion = bf16[768,1536]{1,0:T(8,128)(2,1)} fusion(bf16[256,768]{1,0:T(8,128)(2,1)S(1)} %copy-done.11, bf16[256,1536]{1,0:T(8,128)(2,1)S(1)} %fusion.9), kind=kOutput, calls=%fused_computation.6 | convolution fusion | flops 605159424 | bytes 3538944 | tf_op jit(solution)/shard_map/dot_general | solution.py:174
  130.3 4.3 %copy.24 = bf16[768,1536]{0,1:T(8,128)(2,1)} copy(bf16[768,1536]{1,0:T(8,128)(2,1)} %convolution_convert_fusion) | data formatting | bytes 4718592 | tf_op jit(solution)/shard_map/convert_element_type | solution.py:269
  134.6 4.2 %copy.25 = bf16[768,4,384]{2,0,1:T(8,128)(2,1)} copy(bf16[768,4,384]{0,2,1:T(8,128)(2,1)} %bitcast.198) | data formatting | bytes 4718592 | tf_op jit(solution)/shard_map/reshape | solution.py:271
  138.8 1.7 copy-done.1
  140.5 29.6 %shard_map.118 = bf16[768,384]{1,0:T(8,128)(2,1)S(1)} custom-call(bf16[4,768,384]{2,1,0:T(8,128)(2,1)S(1)} %bitcast.193), custom_call_target="tpu_custom_call" | custom-call | tf_op jit(solution)/shard_map/pallas_call | solution.py:103
  170.1 17.3 %shard_map.119.x_ref = bf16[96,384]{1,0:T(8,128)(2,1)S(1)} custom-call(bf16[8,96,384]{2,1,0:T(8,128)(2,1)S(1)} %bitcast.195), custom_call_target="tpu_custom_call" | custom-call | tf_op jit(solution)/shard_map/pallas_call | solution.py:103
  187.4 6.1 %shard_map.120 = bf16[4,96,384]{2,1,0:T(8,128)(2,1)S(1)} custom-call(bf16[96,384]{1,0:T(8,128)(2,1)S(1)} %shard_map.119.x_ref), custom_call_target="tpu_custom_call" | custom-call | tf_op jit(solution)/shard_map/pallas_call | solution.py:103
  194.5 2.6 %fusion.10 = f32[256,1536]{1,0:T(8,128)S(1)} fusion(bf16[3,1536,768]{2,1,0:T(8,128)(2,1)} %param.12, bf16[256,768]{1,0:T(8,128)(2,1)S(1)} %copy-done.14, bf16[16,768]{1,0:T(8,128)(2,1)S(1)} %collective-permute-done.4), kind=kOutput, calls=%fused_computation.23 | convolution fusion | flops 604766208 | bytes 4349952 | tf_op jit(solution)/shard_map/dot_general | solution.py:174
  197.2 3.1 %fusion.55 = (f32[256]{0:T(256)S(1)}, f32[256,1536]{1,0:T(8,128)S(1)}) fusion(bf16[1,256,1536]{2,1,0:T(8,128)(2,1)S(1)} %copy-done.3, f32[1536]{0:T(1024)S(1)} %copy-done.12, f32[256]{0:T(256)S(1)} %get-tuple-element.11, f32[256,1536]{1,0:T(8,128)S(1)} %fusion.10, f32[256,1536]{1,0:T(8,128)S(1)} %copy-done.21, bf16[3,1536,768]{2,1,0:T(8,128)(2,1)} %param.12, ...), kind=kOutput, calls=%fused_computation.70 | convolution fusion | flops 611450624 | bytes 8290304 | tf_op jit(solution)/shard_map/dot_general | solution.py:174
  200.3 1.4 fusion.109
  (90 shorter events, 13.0 us)
Async XLA Ops:
  0.6 35.1 %copy-start = (bf16[768,1536]{1,0:T(8,128)(2,1)S(1)}, bf16[768,1536]{1,0:T(8,128)(2,1)}, u32[]{:S(2)}) copy-start(bf16[768,1536]{1,0:T(8,128)(2,1)} %param.13) | copy-start | bytes 7077892
  0.6 13.5 %copy-start.9 = (f32[1,4,4096]{2,1,0:T(4,128)S(1)}, f32[1,4,4096]{2,1,0:T(4,128)}, u32[]{:S(2)}) copy-start(f32[1,4,4096]{2,1,0:T(4,128)} %param.19) | copy-start | bytes 196612
  0.7 13.7 %copy-start.20 = (s32[1,16]{1,0:T(1,128)S(1)}, s32[1,16]{1,0:T(1,128)}, u32[]{:S(2)}) copy-start(s32[1,16]{1,0:T(1,128)} %param.18) | copy-start | bytes 196
  0.7 13.8 %copy-start.19 = (s32[1,16]{1,0:T(1,128)S(1)}, s32[1,16]{1,0:T(1,128)}, u32[]{:S(2)}) copy-start(s32[1,16]{1,0:T(1,128)} %param.17) | copy-start | bytes 196
  2.2 18.8 %copy-start.2 = (bf16[1,256,1536]{2,1,0:T(8,128)(2,1)S(1)}, bf16[1,256,1536]{2,1,0:T(8,128)(2,1)}, u32[]{:S(2)}) copy-start(bf16[1,256,1536]{2,1,0:T(8,128)(2,1)} %param.10) | copy-start | bytes 2359300
  2.2 18.8 %copy-start.12 = (f32[1536]{0:T(1024)S(1)}, f32[1536]{0:T(1024)}, u32[]{:S(2)}) copy-start(f32[1536]{0:T(1024)} %param.11) | copy-start | bytes 18436
  8.5 22.4 %collective-permute-start = (bf16[16,1536]{1,0:T(8,128)(2,1)S(1)}, bf16[16,1536]{1,0:T(8,128)(2,1)}, u32[]{:S(2)}, u32[]{:S(2)}) collective-permute-start(bf16[16,1536]{1,0:T(8,128)(2,1)S(1)} %get-tuple-element.2), channel_id=1, source_target_pairs={{0,8},{8,16},{16,24},{1,9},{9,17},{17,25},{2,10},{10,18},{18,26},{... | collective-permute-start | bytes 147464 | tf_op jit(solution)/shard_map/ppermute | solution.py:161
  9.8 18.3 %collective-permute-start.1 = (bf16[16,1536]{1,0:T(8,128)(2,1)S(1)}, bf16[16,1536]{1,0:T(8,128)(2,1)}, u32[]{:S(2)}, u32[]{:S(2)}) collective-permute-start(bf16[16,1536]{1,0:T(8,128)(2,1)S(1)} %get-tuple-element.3), channel_id=1, source_target_pairs={{8,0},{16,8},{24,16},{9,1},{17,9},{25,17},{10,2},{18,10},{26,18},{... | collective-permute-start | bytes 147464 | tf_op jit(solution)/shard_map/ppermute | solution.py:162
  21.0 6.9 %copy-start.17 = (s32[1,16,8]{1,2,0:T(8,128)S(1)}, s32[1,16,8]{1,2,0:T(8,128)}, u32[]{:S(2)}) copy-start(s32[1,16,8]{1,2,0:T(8,128)} %param.16) | copy-start | bytes 1540
  27.7 9.8 %copy-start.16 = (s32[256]{0:T(256)}, s32[256]{0:T(256)S(1)}, u32[]{:S(2)}) copy-start(s32[256]{0:T(256)S(1)} %iota_add_fusion) | copy-start | bytes 3076
  28.0 9.5 %copy-start.15 = (s32[128]{0:T(128)}, s32[128]{0:T(128)S(1)}, u32[]{:S(2)}) copy-start(s32[128]{0:T(128)S(1)} %eq.53) | copy-start | bytes 1540
  28.0 2.8 %copy-start.6 = (bf16[256,1536]{1,0:T(8,128)(2,1)S(1)}, bf16[256,1536]{1,0:T(8,128)(2,1)}, u32[]{:S(2)}) copy-start(bf16[256,1536]{1,0:T(8,128)(2,1)} %copy-done.5) | copy-start | bytes 2359300
  28.0 2.8 %copy-start.23 = (f32[256,768]{1,0:T(8,128)S(1)}, f32[256,768]{1,0:T(8,128)}, u32[]{:S(2)}) copy-start(f32[256,768]{1,0:T(8,128)} %fusion.16) | copy-start | bytes 2359300
  36.6 46.8 %copy-start.7 = (bf16[256,1536]{1,0:T(8,128)(2,1)}, bf16[256,1536]{1,0:T(8,128)(2,1)S(1)}, u32[]{:S(2)}) copy-start(bf16[256,1536]{1,0:T(8,128)(2,1)S(1)} %fusion.8) | copy-start | bytes 2359300
  36.6 46.2 %copy-start.4 = (bf16[1536,512]{1,0:T(8,128)(2,1)S(1)}, bf16[1536,512]{1,0:T(8,128)(2,1)}, u32[]{:S(2)}) copy-start(bf16[1536,512]{1,0:T(8,128)(2,1)} %param.14) | copy-start | bytes 4718596
  36.6 76.8 %collective-permute-start.2 = (bf16[256,1536]{1,0:T(8,128)(2,1)S(1)}, bf16[256,1536]{1,0:T(8,128)(2,1)}, u32[]{:S(2)}, u32[]{:S(2)}) collective-permute-start(bf16[256,1536]{1,0:T(8,128)(2,1)S(1)} %fusion.8), channel_id=1, source_target_pairs={{0,24},{8,16},{16,8},{24,0},{1,25},{9,17},{17,9},{25,1},{2,26},{10... | collective-permute-start | bytes 2359304 | tf_op jit(solution)/shard_map/ppermute | solution.py:227
  84.1 29.3 %copy-start.8 = (bf16[256,1536]{1,0:T(8,128)(2,1)S(1)}, bf16[256,1536]{1,0:T(8,128)(2,1)}, u32[]{:S(2)}) copy-start(bf16[256,1536]{1,0:T(8,128)(2,1)} %copy-done.7) | copy-start | bytes 2359300
  121.6 3.9 %copy-start.13 = (bf16[256,768]{1,0:T(8,128)(2,1)}, bf16[256,768]{1,0:T(8,128)(2,1)S(1)}, u32[]{:S(2)}) copy-start(bf16[256,768]{1,0:T(8,128)(2,1)S(1)} %fusion.99) | copy-start | bytes 1179652
  121.6 3.8 %copy-start.11 = (bf16[256,768]{1,0:T(8,128)(2,1)S(1)}, bf16[256,768]{1,0:T(8,128)(2,1)}, u32[]{:S(2)}) copy-start(bf16[256,768]{1,0:T(8,128)(2,1)} %copy-done.10) | copy-start | bytes 1179652
  127.7 69.4 %collective-permute-start.3 = (bf16[16,768]{1,0:T(8,128)(2,1)S(1)}, bf16[16,768]{1,0:T(8,128)(2,1)S(1)}, u32[]{:S(2)}, u32[]{:S(2)}) collective-permute-start(bf16[16,768]{1,0:T(8,128)(2,1)S(1)} %get-tuple-element.4), channel_id=1, source_target_pairs={{8,0},{16,8},{24,16},{9,1},{17,9},{25,17},{10,2},{18,10},{26,18},{... | collective-permute-start | bytes 73736 | tf_op jit(solution)/shard_map/ppermute | solution.py:162
  129.0 65.5 %collective-permute-start.4 = (bf16[16,768]{1,0:T(8,128)(2,1)S(1)}, bf16[16,768]{1,0:T(8,128)(2,1)S(1)}, u32[]{:S(2)}, u32[]{:S(2)}) collective-permute-start(bf16[16,768]{1,0:T(8,128)(2,1)S(1)} %get-tuple-element.5), channel_id=1, source_target_pairs={{0,8},{8,16},{16,24},{1,9},{9,17},{17,25},{2,10},{10,18},{18,26},{... | collective-permute-start | bytes 73736 | tf_op jit(solution)/shard_map/ppermute | solution.py:161
  170.1 24.4 %copy-start.14 = (bf16[256,768]{1,0:T(8,128)(2,1)S(1)}, bf16[256,768]{1,0:T(8,128)(2,1)}, u32[]{:S(2)}) copy-start(bf16[256,768]{1,0:T(8,128)(2,1)} %copy-done.13) | copy-start | bytes 1179652
  194.5 2.7 %copy-start.21 = (f32[256,1536]{1,0:T(8,128)S(1)}, f32[256,1536]{1,0:T(8,128)}, u32[]{:S(2)}) copy-start(f32[256,1536]{1,0:T(8,128)} %fusion.14) | copy-start | bytes 4718596
  197.1 3.2 %copy-start.18 = (f32[256]{0:T(256)S(1)}, f32[256]{0:T(256)}, u32[]{:S(2)}) copy-start(f32[256]{0:T(256)} %get-tuple-element.10) | copy-start | bytes 3076
  (5 other events, 8.0 us)

commit v2 on v1

--- a/solution.py
+++ b/solution.py
@@ -13,22 +13,28 @@
 F32 = jnp.float32
 
 
-def greet(axis, count):
-    me = lax.axis_index(axis)
+def place(axis, stride):
+    index = lax.axis_index(axis)
+    me = lax.div(index, stride)
+    rest = lax.rem(index, stride)
+    return me, lambda at: at * stride + rest
+
+
+def greet(axis, devices):
     barrier = pltpu.get_barrier_semaphore()
-    for step in range(1, count):
-        pl.semaphore_signal(
-            barrier,
-            inc=1,
-            device_id={axis: lax.rem(me + step, count)},
-            device_id_type=MESH,
-        )
-    pl.semaphore_wait(barrier, count - 1)
-    return me
-
-
-def exchange_kernel(axis, count, x_ref, o_ref, local, send_sem, recv_sem):
-    me = greet(axis, count)
+    for device in devices:
+        pl.semaphore_signal(barrier, inc=1, device_id={axis: device}, device_id_type=MESH)
+    pl.semaphore_wait(barrier, len(devices))
+
+
+def join(axis, stride, count):
+    me, at = place(axis, stride)
+    greet(axis, [at(lax.rem(me + step, count)) for step in range(1, count)])
+    return me, at
+
+
+def exchange_kernel(axis, stride, count, x_ref, o_ref, local, send_sem, recv_sem):
+    me, at = join(axis, stride, count)
     copies = []
     for step in range(1, count):
         peer = lax.rem(me + step, count)
@@ -37,7 +43,7 @@
             dst_ref=o_ref.at[me],
             send_sem=send_sem.at[step],
             recv_sem=recv_sem.at[step],
-            device_id={axis: peer},
+            device_id={axis: at(peer)},
             device_id_type=MESH,
         )
         copy.start()
@@ -49,8 +55,8 @@
         copy.wait()
 
 
-def gather_kernel(axis, count, x_ref, o_ref, local, send_sem, recv_sem):
-    me = greet(axis, count)
+def gather_kernel(axis, stride, count, x_ref, o_ref, local, send_sem, recv_sem):
+    me, at = join(axis, stride, count)
     copies = []
     for step in range(1, count):
         peer = lax.rem(me + step, count)
@@ -59,7 +65,7 @@
             dst_ref=o_ref.at[me],
             send_sem=send_sem.at[step],
             recv_sem=recv_sem.at[step],
-            device_id={axis: peer},
+            device_id={axis: at(peer)},
             device_id_type=MESH,
         )
         copy.start()
@@ -71,8 +77,8 @@
         copy.wait()
 
 
-def reduce_kernel(axis, count, x_ref, o_ref, held, send_sem, recv_sem):
-    me = greet(axis, count)
+def reduce_kernel(axis, stride, count, x_ref, o_ref, held, send_sem, recv_sem):
+    me, at = join(axis, stride, count)
     copies = []
     for step in range(1, count):
         peer = lax.rem(me + step, count)
@@ -81,7 +87,7 @@
             dst_ref=held.at[step],
             send_sem=send_sem.at[step],
             recv_sem=recv_sem.at[step],
-            device_id={axis: peer},
+            device_id={axis: at(peer)},
             device_id_type=MESH,
         )
         copy.start()
@@ -118,10 +124,10 @@
     )(x)
 
 
-def exchange(x, axis, cid):
-    count = lax.axis_size(axis)
+def exchange(x, axis, cid, stride=1):
+    count = lax.axis_size(axis) // stride
     return run(
-        functools.partial(exchange_kernel, axis, count),
+        functools.partial(exchange_kernel, axis, stride, count),
         x,
         jax.ShapeDtypeStruct(x.shape, x.dtype),
         pltpu.SemaphoreType.DMA,
@@ -130,10 +136,10 @@
     )
 
 
-def gather(x, axis, cid):
-    count = lax.axis_size(axis)
+def gather(x, axis, cid, stride=1):
+    count = lax.axis_size(axis) // stride
     return run(
-        functools.partial(gather_kernel, axis, count),
+        functools.partial(gather_kernel, axis, stride, count),
         x,
         jax.ShapeDtypeStruct((count,) + x.shape, x.dtype),
         pltpu.SemaphoreType.DMA,
@@ -142,16 +148,87 @@
     )
 
 
-def reduce_pieces(x, axis, cid):
-    count = lax.axis_size(axis)
+def reduce_pieces(x, axis, cid, stride=1):
+    count = lax.axis_size(axis) // stride
     return run(
-        functools.partial(reduce_kernel, axis, count),
+        functools.partial(reduce_kernel, axis, stride, count),
         x,
         jax.ShapeDtypeStruct(x.shape[1:], x.dtype),
         pltpu.VMEM(x.shape, x.dtype),
         cid,
         count,
     )
+
+
+def weight_kernel(
+    axis, count, a_ref, g_ref, o_ref, out1, in1, out2, in2, send1, recv1, send2, recv2
+):
+    me = lax.axis_index(axis)
+    half = count // 2
+    spot, parity = lax.div(me, 2), lax.rem(me, 2)
+    buddy = 2 * spot + 1 - parity
+    quarters = [lax.rem(spot + step, half) for step in range(half)]
+    greet(axis, [buddy] + [2 * quarters[step] + parity for step in range(1, half)])
+
+    def term(part):
+        return lax.dot_general(
+            a_ref[...], g_ref[part], (((0,), (0,)), ((), ())), preferred_element_type=F32
+        )
+
+    order = list(range(1, half)) + [0]
+    first = {}
+    for step in order:
+        out1[step] = term(2 * quarters[step] + 1 - parity).astype(BF)
+        first[step] = pltpu.make_async_remote_copy(
+            src_ref=out1.at[step],
+            dst_ref=in1.at[step],
+            send_sem=send1.at[step],
+            recv_sem=recv1.at[step],
+            device_id={axis: buddy},
+            device_id_type=MESH,
+        )
+        first[step].start()
+    second = {}
+    for step in order:
+        total = term(2 * quarters[step] + parity)
+        first[step].wait_recv()
+        total = total + in1[step].astype(F32)
+        if step:
+            out2[step] = total.astype(BF)
+            second[step] = pltpu.make_async_remote_copy(
+                src_ref=out2.at[step],
+                dst_ref=in2.at[step],
+                send_sem=send2.at[step],
+                recv_sem=recv2.at[step],
+                device_id={axis: 2 * quarters[step] + parity},
+                device_id_type=MESH,
+            )
+            second[step].start()
+    for step in range(1, half):
+        second[step].wait_recv()
+        total = total + in2[step].astype(F32)
+    o_ref[...] = total.astype(o_ref.dtype)
+    for step in range(half):
+        first[step].wait_send()
+    for step in range(1, half):
+        second[step].wait_send()
+
+
+def weight_sum(active, grad, axis, cid):
+    count, rows, wide = grad.shape
+    hid = active.shape[1]
+    half = count // 2
+    return pl.pallas_call(
+        functools.partial(weight_kernel, axis, count),
+        out_shape=jax.ShapeDtypeStruct((hid, wide), BF),
+        in_specs=[vmem(), vmem()],
+        out_specs=vmem(),
+        scratch_shapes=[pltpu.VMEM((half, hid, wide), BF) for _ in range(4)]
+        + [pltpu.SemaphoreType.DMA((half,)) for _ in range(4)],
+        compiler_params=pltpu.CompilerParams(
+            collective_id=cid, has_side_effects=True, vmem_limit_bytes=32 * 1024 * 1024
+        ),
+    )(active, grad)
 
 
 def with_halo(block, axis, width):
@@ -197,19 +274,24 @@
     part = head_weight.shape[1]
     own_rows = own_genes * exons
 
+    other_head = lax.ppermute(
+        head_weight, "batch", [(i, i ^ 1) for i in range(batch_devices)]
+    )
     own_strand = lax.dynamic_slice_in_dim(gene_strand[0], bin_index * own_genes, own_genes, 0)
     own_count = lax.dynamic_slice_in_dim(exon_count[0], bin_index * own_genes, own_genes, 0)
     target = gene_target[0]
     lane = lax.broadcasted_iota(jnp.int32, target.shape, 1)
     swapped = jnp.where(lane % 2 == 0, jnp.roll(target, -1, axis=1), jnp.roll(target, 1, axis=1))
     target = jnp.where(own_strand[:, None] == 1, swapped, target)
-    pieces = target.reshape(own_genes, batch_devices, part).transpose(1, 0, 2)
-    counted = jnp.broadcast_to(
-        own_count.astype(F32)[None, :, None], (batch_devices, own_genes, 128)
-    )
-    arrived = exchange(jnp.concatenate([pieces, counted], axis=2), "batch", 1)
-    track_target = arrived[:, :, :part]
-    track_count = arrived[:, :, part : part + 1].astype(jnp.int32)
+    pairs = batch_devices // 2
+    odd = lax.rem(lax.axis_index("batch"), 2)
+    pieces = target.reshape(own_genes, pairs, 2, part)
+    pieces = jnp.where(odd == 1, pieces[:, :, ::-1], pieces)
+    pieces = pieces.reshape(own_genes, pairs, 2 * part).transpose(1, 0, 2)
+    counted = jnp.broadcast_to(own_count.astype(F32)[None, :, None], (pairs, own_genes, 128))
+    arrived = exchange(jnp.concatenate([pieces, counted], axis=2), "batch", 1, 2)
+    track_target = arrived[:, :, : 2 * part]
+    track_count = arrived[:, :, 2 * part : 2 * part + 1].astype(jnp.int32)
 
     widened = features[0].astype(F32)
     inverse = lax.rsqrt(jnp.mean(widened * widened, axis=-1, keepdims=True) + 1e-06)
@@ -224,10 +306,6 @@
     active = jax.nn.gelu(conv_sum, approximate=False).astype(BF)
     block_out = (widened + dot(active, out_weight)).astype(BF)
 
-    partner = lax.ppermute(
-        block_out, "bins", [(i, bin_devices - 1 - i) for i in range(bin_devices)]
-    )
-
     positions = bin_index * rows + jnp.arange(rows, dtype=jnp.int32)
     listed = jnp.arange(exons, dtype=jnp.int32)[None, :] < exon_count[0][:, None]
     hits = (
@@ -235,18 +313,25 @@
     ).reshape(genes * exons, rows).astype(BF)
     picked = dot(hits, block_out).astype(BF).reshape(bin_devices, own_rows, channels)
     own_picked = reduce_pieces(picked, "bins", 2)
-    all_picked = gather(own_picked, "batch", 3).reshape(batch_devices * own_rows, channels)
-
-    logits = dot(all_picked, head_weight).reshape(batch_devices, own_genes, exons, part)
+    own_picked, block_out = lax.optimization_barrier((own_picked, block_out))
+    partner = lax.ppermute(
+        block_out, "bins", [(i, bin_devices - 1 - i) for i in range(bin_devices)]
+    )
+    all_picked = gather(own_picked, "batch", 3, 2).reshape(pairs * own_rows, channels)
+
+    logits = jnp.concatenate([dot(all_picked, head_weight), dot(all_picked, other_head)], axis=1)
+    logits = logits.reshape(pairs, own_genes, exons, 2 * part)
     predicted = jax.nn.softplus(logits).astype(BF).astype(F32)
     counts = lax.broadcasted_iota(jnp.int32, (1, 1, exons, 1), 2) < track_count[..., None]
     partial = jnp.sum(jnp.where(counts, predicted, 0.0), axis=2)
     spread = (1.0 - track_target / (1.0 + partial)).astype(BF).astype(F32)
     logit_grad = jnp.where(counts, spread[:, :, None, :] * jax.nn.sigmoid(logits), 0.0).astype(BF)
-    picked_grad = dot(
-        logit_grad.reshape(batch_devices * own_rows, part), head_weight, ((1,), (1,))
-    ).astype(BF).reshape(batch_devices, own_rows, channels)
-    own_grad = reduce_pieces(picked_grad, "batch", 4)
+    logit_grad = logit_grad.reshape(pairs * own_rows, 2 * part)
+    picked_grad = dot(logit_grad[:, :part], head_weight, ((1,), (1,))) + dot(
+        logit_grad[:, part:], other_head, ((1,), (1,))
+    )
+    picked_grad = picked_grad.astype(BF).reshape(pairs, own_rows, channels)
+    own_grad = reduce_pieces(picked_grad, "batch", 4, 2)
     seq_grad = gather(own_grad, "bins", 5).reshape(genes * exons, channels)
     head_back = dot(hits, seq_grad, ((0,), (0,)))
 
@@ -266,10 +351,10 @@
     act_grad = (dot(block_grad, out_weight, ((1,), (1,))) * gelu_slope(conv_sum)).astype(BF)
     padded_grad = with_halo(act_grad, "bins", DILATION_STEP)
 
-    weight_terms = dot(active, block_grad, ((0,), (0,))).astype(BF)
     wide = channels // bin_devices
-    weight_terms = weight_terms.reshape(hid, bin_devices, wide).transpose(1, 0, 2)
-    bins_sum = reduce_pieces(weight_terms, "bins", 6)
+    bins_sum = weight_sum(
+        active, block_grad.reshape(rows, bin_devices, wide).transpose(1, 0, 2), "bins", 6
+    )
     own_sum = reduce_pieces(
         bins_sum.reshape(batch_devices, hid // batch_devices, wide), "batch", 7
     )

time: 202 us -> 161 us (0.80)
  Pallas kernels: 132 us -> 84.7 us
  matrix products: 36.7 us -> 43.5 us
  local copies, waits for them, and re-layouts: 12.7 us -> 8.75 us
  other arithmetic: 10.1 us -> 12.3 us
    pallas_call x8 -> x7, Pallas kernels: 132 us -> 68.9 us  [run(): pl.pallas_call(kernel, out_shape=out, in_specs=[vmem()], out_specs=vmem()...]
    pallas_call x0 -> x1, Pallas kernels: none -> 15.8 us  [weight_sum(): pl.pallas_call(functools.partial(weight_kernel, axis, count), out_shape=j...]
    dot_general x14 -> x15, matrix products: 36.7 us -> 43.5 us  [dot(): return lax.dot_general(a, b, (dims, ((), ())), preferred_element_type=F32)]
    convert_element_type x2 -> x1, local copies, waits for them, and re-layouts: 4.39 us -> 1.18 us  [per_device(): block_grad = (head_back + rc_grad).astype(BF)]
    reshape x1 -> x2, local copies, waits for them, and re-layouts: 4.25 us -> 2.18 us  [the longest x1 1.48 us: per_device(): block_grad.reshape(rows, bin_devices, wide).transpose(1, 0, 2)]
  transfers between devices with their start and end apart: 5 -> 6, of which waited for: 0 -> 0; matrix products, arithmetic and copies ran while one was open for 13% -> 22% of each run, Pallas kernels for 66% -> 16%
where the time goes in v2:
time: 161 us; the launch traced here: 160 us
  Pallas kernels  84.7 us (53%)
  matrix products  43.5 us (27%)
  other arithmetic  12.3 us (8%)
  starting transfers between devices  9.31 us (6%)
  local copies, waits for them, and re-layouts  8.75 us (5%)
    pallas_call x7, Pallas kernels, run(): pl.pallas_call(kernel, out_shape=out, in_specs=[vmem()], out_specs=vmem()...  68.9 us
    dot_general x15, matrix products, dot(): return lax.dot_general(a, b, (dims, ((), ())), preferred_element_type=F32)  43.5 us
    pallas_call x1, Pallas kernels, weight_sum(): pl.pallas_call(functools.partial(weight_kernel, axis, count), out_shape=j...  15.8 us
    ppermute x2, starting transfers between devices, with_halo(): high = lax.ppermute(block[:width], axis, backward)  6.35 us
    convert_element_type x1, other arithmetic, per_device(): hidden = jax.nn.gelu(normed, approximate=False).astype(BF)  4.84 us
  transfers between devices with their start and end apart: 6, of which 0 were waited for; matrix products, arithmetic and copies ran while one was open for 22% of the time, Pallas kernels for 16%

profile of v2, /device:TPU:15, one launch (start us, length us, event | category | flops | bytes accessed | tf_op | source)
XLA Modules:
  0.0 159.8 jit_solution(13726984746211359505)
XLA Ops:
  3.3 4.8 %fusion.39 = bf16[256,1536]{1,0:T(8,128)(2,1)S(1)} fusion(bf16[1,256,1536]{2,1,0:T(8,128)(2,1)} %param.10, f32[1536]{0:T(1024)} %param.11, f32[256]{0:T(256)S(1)} %get-tuple-element.15), kind=kLoop, calls=%fused_computation.53 | loop fusion | flops 26738688 | bytes 1580032 | tf_op jit(solution)/shard_map/convert_element_type | solution.py:299
  9.7 3.2 %collective-permute-start.1 = (bf16[16,1536]{1,0:T(8,128)(2,1)}, bf16[16,1536]{1,0:T(8,128)(2,1)}, u32[]{:S(2)}, u32[]{:S(2)}) collective-permute-start(bf16[16,1536]{1,0:T(8,128)(2,1)} %get-tuple-element.7), channel_id=1, source_target_pairs={{8,0},{16,8},{24,16},{9,1},{17,9},{25,17},{10,2},{18,10},{26,18},{... | collective-permute-start | bytes 147464 | tf_op jit(solution)/shard_map/ppermute | solution.py:239
  18.7 6.8 %fusion.17 = f32[256,768]{1,0:T(8,128)} fusion(bf16[3,1536,768]{2,1,0:T(8,128)(2,1)} %param.12, bf16[1,256,1536]{2,1,0:T(8,128)(2,1)S(1)} %copy-done.1, f32[1536]{0:T(1024)} %param.11, f32[256]{0:T(256)} %copy-done.13), kind=kOutput, calls=%fused_computation.29 | convolution fusion | flops 630718464 | bytes 3941376 | tf_op jit(solution)/shard_map/dot_general | solution.py:251
  26.7 2.8 %fusion.13 = f32[256,768]{1,0:T(8,128)S(1)} fusion(bf16[3,1536,768]{2,1,0:T(8,128)(2,1)} %param.12, bf16[16,1536]{1,0:T(8,128)(2,1)} %collective-permute-done.1, bf16[256,1536]{1,0:T(8,128)(2,1)} %copy-done.7), kind=kOutput, calls=%fused_computation.25 | convolution fusion | flops 605552640 | bytes 3981312 | tf_op jit(solution)/shard_map/dot_general | solution.py:251
  29.5 4.9 %fusion.101 = (bf16[256,768]{1,0:T(8,128)(2,1)S(1)}, f32[256,768]{1,0:T(8,128)}) fusion(f32[256,768]{1,0:T(8,128)S(1)} %fusion.13, f32[256,768]{1,0:T(8,128)S(1)} %copy-done.23, bf16[3,1536,768]{2,1,0:T(8,128)(2,1)} %param.12, bf16[256,1536]{1,0:T(8,128)(2,1)S(1)} %copy-done.8, bf16[16,1536]{1,0:T(8,128)(2,1)} %collective-permute-done), kind=kOutput, calls=%fused_computation.115 | convolution fusion | flops 618725376 | bytes 5947392 | tf_op jit(solution)/shard_map/dot_general | solution.py:251
  34.4 1.7 %fusion.8 = bf16[256,1536]{1,0:T(8,128)(2,1)} fusion(bf16[256,768]{1,0:T(8,128)(2,1)S(1)} %get-tuple-element.16.a_ref, bf16[768,1536]{1,0:T(8,128)(2,1)S(1)} %copy-done, bf16[1,256,1536]{2,1,0:T(8,128)(2,1)S(1)} %copy-done.1), kind=kOutput, calls=%fused_computation.14 | convolution fusion | flops 605159424 | bytes 4325376 | tf_op jit(solution)/shard_map/dot_general | solution.py:251
  37.6 8.5 %shard_map.114.x_ref = bf16[32,1536]{1,0:T(8,128)(2,1)S(1)} custom-call(bf16[4,32,1536]{2,1,0:T(8,128)(2,1)S(1)} %bitcast.196), custom_call_target="tpu_custom_call" | custom-call | tf_op jit(solution)/shard_map/pallas_call | solution.py:109
  46.3 5.2 %shard_map.113 = f32[4,4,1152]{2,1,0:T(4,128)S(1)} custom-call(f32[4,4,1152]{2,1,0:T(4,128)S(1)} %pad_maximum_fusion.9.x_ref), custom_call_target="tpu_custom_call" | custom-call | tf_op jit(solution)/shard_map/pallas_call | solution.py:109
  51.8 12.2 %shard_map.115 = bf16[4,32,1536]{2,1,0:T(8,128)(2,1)S(1)} custom-call(bf16[32,1536]{1,0:T(8,128)(2,1)S(1)} %shard_map.114.x_ref), custom_call_target="tpu_custom_call" | custom-call | tf_op jit(solution)/shard_map/pallas_call | solution.py:109
  64.0 2.5 %fusion.206 = f32[128,512]{1,0:T(8,128)} fusion(bf16[128,1536]{1,0:T(8,128)(2,1)S(1)} %bitcast.191, bf16[1536,512]{1,0:T(8,128)(2,1)} %param.14), kind=kOutput, calls=%fused_computation.256 | convolution fusion | flops 201326592 | bytes 2228224 | tf_op jit(solution)/shard_map/dot_general | solution.py:251
  66.5 5.6 %fusion.7 = f32[256,1536]{1,0:T(8,128)} fusion(s32[1536]{0:T(1024)S(1)} %copy-done.21, bf16[256,1536]{1,0:T(8,128)(2,1)} %fusion.8, bf16[256,1536]{1,0:T(8,128)(2,1)} %collective-permute-done.3, s32[256]{0:T(256)S(1)} %iota_subtract_fusion), kind=kOutput, calls=%fused_computation.13 | convolution fusion | flops 1425080320 | bytes 3152896 | tf_op jit(solution)/shard_map/dot_general | solution.py:251
  72.1 1.8 %fusion.207 = f32[128,512]{1,0:T(8,128)S(1)} fusion(bf16[128,1536]{1,0:T(8,128)(2,1)S(1)} %bitcast.192, bf16[1536,512]{1,0:T(8,128)(2,1)} %collective-permute-done.2), kind=kOutput, calls=%fused_computation.257 | convolution fusion | flops 201326592 | bytes 2228224 | tf_op jit(solution)/shard_map/dot_general | solution.py:251
  74.6 2.0 %fusion.156 = f32[128,1536]{1,0:T(8,128)S(1)} fusion(bf16[1536,512]{1,0:T(8,128)(2,1)} %param.14, bf16[128,1024]{1,0:T(8,128)(2,1)S(1)} %fusion.152), kind=kOutput, calls=%fused_computation.186 | convolution fusion | flops 201326592 | bytes 2490368 | tf_op jit(solution)/shard_map/dot_general | solution.py:251
  76.6 2.2 %fusion.10 = bf16[128,1536]{1,0:T(8,128)(2,1)S(1)} fusion(f32[128,1536]{1,0:T(8,128)S(1)} %fusion.156, bf16[1536,512]{1,0:T(8,128)(2,1)} %collective-permute-done.2, bf16[128,1024]{1,0:T(8,128)(2,1)S(1)} %fusion.152), kind=kOutput, calls=%fused_computation.18 | convolution fusion | flops 201719808 | bytes 2883584 | tf_op jit(solution)/shard_map/dot_general | solution.py:251
  78.8 9.9 %shard_map.116.x_ref = bf16[32,1536]{1,0:T(8,128)(2,1)S(1)} custom-call(bf16[4,32,1536]{2,1,0:T(8,128)(2,1)S(1)} %bitcast.197), custom_call_target="tpu_custom_call" | custom-call | tf_op jit(solution)/shard_map/pallas_call | solution.py:109
  88.8 8.4 %shard_map.117 = bf16[4,32,1536]{2,1,0:T(8,128)(2,1)S(1)} custom-call(bf16[32,1536]{1,0:T(8,128)(2,1)S(1)} %shard_map.116.x_ref), custom_call_target="tpu_custom_call" | custom-call | tf_op jit(solution)/shard_map/pallas_call | solution.py:109
  98.9 2.0 %fusion.98 = bf16[256,768]{1,0:T(8,128)(2,1)S(1)} fusion(bf16[256,1536]{1,0:T(8,128)(2,1)S(1)} %fusion.9, bf16[768,1536]{1,0:T(8,128)(2,1)S(1)} %copy-done, f32[256,768]{1,0:T(8,128)} %get-tuple-element.17), kind=kOutput, calls=%fused_computation.110 | convolution fusion | flops 605945856 | bytes 4325376 | tf_op jit(solution)/shard_map/dot_general | solution.py:251
  101.6 3.7 %fusion.15 = f32[256,1536]{1,0:T(8,128)} fusion(bf16[256,768]{1,0:T(8,128)(2,1)S(1)} %fusion.98, bf16[3,1536,768]{2,1,0:T(8,128)(2,1)} %param.12), kind=kOutput, calls=%fused_computation.27 | convolution fusion | flops 603979776 | bytes 4325376 | tf_op jit(solution)/shard_map/dot_general | solution.py:251
  106.8 15.8 %shard_map.118 = bf16[768,384]{1,0:T(8,128)(2,1)S(1)} custom-call(bf16[256,768]{1,0:T(8,128)(2,1)S(1)} %get-tuple-element.16.a_ref, bf16[4,256,384]{2,1,0:T(8,128)(2,1)S(1)} %bitcast.193), custom_call_target="tpu_custom_call" | custom-call | tf_op jit(solution)/shard_map/pallas_call | solution.py:221
  122.6 18.5 %shard_map.119.x_ref = bf16[96,384]{1,0:T(8,128)(2,1)S(1)} custom-call(bf16[8,96,384]{2,1,0:T(8,128)(2,1)S(1)} %bitcast.194), custom_call_target="tpu_custom_call" | custom-call | tf_op jit(solution)/shard_map/pallas_call | solution.py:109
  141.1 6.1 %shard_map.120 = bf16[4,96,384]{2,1,0:T(8,128)(2,1)S(1)} custom-call(bf16[96,384]{1,0:T(8,128)(2,1)S(1)} %shard_map.119.x_ref), custom_call_target="tpu_custom_call" | custom-call | tf_op jit(solution)/shard_map/pallas_call | solution.py:109
  149.4 3.2 %collective-permute-start.4 = (bf16[16,768]{1,0:T(8,128)(2,1)S(1)}, bf16[16,768]{1,0:T(8,128)(2,1)S(1)}, u32[]{:S(2)}, u32[]{:S(2)}) collective-permute-start(bf16[16,768]{1,0:T(8,128)(2,1)S(1)} %copy-done.11), channel_id=1, source_target_pairs={{8,0},{16,8},{24,16},{9,1},{17,9},{25,17},{10,2},{18,10},{26,18},{... | collective-permute-start | bytes 73736 | tf_op jit(solution)/shard_map/ppermute | solution.py:239
  152.6 2.5 %fusion.11 = f32[256,1536]{1,0:T(8,128)S(1)} fusion(bf16[3,1536,768]{2,1,0:T(8,128)(2,1)} %param.12, bf16[256,768]{1,0:T(8,128)(2,1)S(1)} %copy-done.17, bf16[16,768]{1,0:T(8,128)(2,1)S(1)} %collective-permute-done.5), kind=kOutput, calls=%fused_computation.23 | convolution fusion | flops 604766208 | bytes 4349952 | tf_op jit(solution)/shard_map/dot_general | solution.py:251
  155.2 3.2 %fusion.56 = (f32[256]{0:T(256)S(1)}, f32[256,1536]{1,0:T(8,128)S(1)}) fusion(bf16[1,256,1536]{2,1,0:T(8,128)(2,1)S(1)} %copy-done.2, f32[1536]{0:T(1024)S(1)} %copy-done.15, f32[256]{0:T(256)S(1)} %copy-done.14, f32[256,1536]{1,0:T(8,128)S(1)} %fusion.11, f32[256,1536]{1,0:T(8,128)S(1)} %copy-done.22, bf16[3,1536,768]{2,1,0:T(8,128)(2,1)} %param.12, ...), kind=kOutput, calls=%fused_computation.70 | convolution fusion | flops 611450624 | bytes 8290304 | tf_op jit(solution)/shard_map/dot_general | solution.py:251
  (98 shorter events, 21.2 us)
Async XLA Ops:
  0.6 33.8 %copy-start = (bf16[768,1536]{1,0:T(8,128)(2,1)S(1)}, bf16[768,1536]{1,0:T(8,128)(2,1)}, u32[]{:S(2)}) copy-start(bf16[768,1536]{1,0:T(8,128)(2,1)} %param.13) | copy-start | bytes 7077892
  0.6 13.8 %copy-start.9 = (f32[1,4,4096]{2,1,0:T(4,128)S(1)}, f32[1,4,4096]{2,1,0:T(4,128)}, u32[]{:S(2)}) copy-start(f32[1,4,4096]{2,1,0:T(4,128)} %param.19) | copy-start | bytes 196612
  3.3 15.4 %copy-start.1 = (bf16[1,256,1536]{2,1,0:T(8,128)(2,1)S(1)}, bf16[1,256,1536]{2,1,0:T(8,128)(2,1)}, u32[]{:S(2)}) copy-start(bf16[1,256,1536]{2,1,0:T(8,128)(2,1)} %param.10) | copy-start | bytes 2359300
  9.7 17.0 %collective-permute-start.1 = (bf16[16,1536]{1,0:T(8,128)(2,1)}, bf16[16,1536]{1,0:T(8,128)(2,1)}, u32[]{:S(2)}, u32[]{:S(2)}) collective-permute-start(bf16[16,1536]{1,0:T(8,128)(2,1)} %get-tuple-element.7), channel_id=1, source_target_pairs={{8,0},{16,8},{24,16},{9,1},{17,9},{25,17},{10,2},{18,10},{26,18},{... | collective-permute-start | bytes 147464 | tf_op jit(solution)/shard_map/ppermute | solution.py:239
  12.9 16.6 %collective-permute-start = (bf16[16,1536]{1,0:T(8,128)(2,1)S(1)}, bf16[16,1536]{1,0:T(8,128)(2,1)}, u32[]{:S(2)}, u32[]{:S(2)}) collective-permute-start(bf16[16,1536]{1,0:T(8,128)(2,1)S(1)} %get-tuple-element.6), channel_id=1, source_target_pairs={{0,8},{8,16},{16,24},{1,9},{9,17},{17,25},{2,10},{10,18},{18,26},{... | collective-permute-start | bytes 147464 | tf_op jit(solution)/shard_map/ppermute | solution.py:238
  14.1 57.9 %collective-permute-start.2 = (bf16[1536,512]{1,0:T(8,128)(2,1)}, bf16[1536,512]{1,0:T(8,128)(2,1)}, u32[]{:S(2)}, u32[]{:S(2)}) collective-permute-start(bf16[1536,512]{1,0:T(8,128)(2,1)} %param.14), channel_id=1, source_target_pairs={{0,1},{1,0},{2,3},{3,2},{4,5},{5,4},{6,7},{7,6},{8,9},{9,8},{10,11... | collective-permute-start | bytes 4718600 | tf_op jit(solution)/shard_map/ppermute | solution.py:277
  18.7 6.8 %copy-start.20 = (s32[1,16]{1,0:T(1,128)S(1)}, s32[1,16]{1,0:T(1,128)}, u32[]{:S(2)}) copy-start(s32[1,16]{1,0:T(1,128)} %param.17) | copy-start | bytes 196
  18.7 7.7 %copy-start.18 = (s32[1,16,8]{1,2,0:T(8,128)S(1)}, s32[1,16,8]{1,2,0:T(8,128)}, u32[]{:S(2)}) copy-start(s32[1,16,8]{1,2,0:T(8,128)} %param.16) | copy-start | bytes 1540
  36.1 10.1 %copy-start.10 = (f32[4,4,1024]{2,0,1:T(4,128)S(1)}, f32[4,4,1024]{2,0,1:T(4,128)}, u32[]{:S(2)}) copy-start(f32[4,4,1024]{2,0,1:T(4,128)} %reshape.160) | copy-start | bytes 196612
  46.1 20.5 %copy-start.21 = (s32[1536]{0:T(1024)S(1)}, s32[1536]{0:T(1024)}, u32[]{:S(2)}) copy-start(s32[1536]{0:T(1024)} %param.15) | copy-start | bytes 18436
  46.1 20.4 %collective-permute-start.3 = (bf16[256,1536]{1,0:T(8,128)(2,1)}, bf16[256,1536]{1,0:T(8,128)(2,1)}, u32[]{:S(2)}, u32[]{:S(2)}) collective-permute-start(bf16[256,1536]{1,0:T(8,128)(2,1)} %fusion.8), channel_id=1, source_target_pairs={{0,24},{8,16},{16,8},{24,0},{1,25},{9,17},{17,9},{25,1},{2,26},{10... | collective-permute-start | bytes 2359304 | tf_op jit(solution)/shard_map/ppermute | solution.py:317
  76.6 20.6 %copy-start.6 = (f32[256,1536]{1,0:T(8,128)S(1)}, f32[256,1536]{1,0:T(8,128)}, u32[]{:S(2)}) copy-start(f32[256,1536]{1,0:T(8,128)} %fusion.7) | copy-start | bytes 4718596
  100.9 4.3 %copy-start.16 = (bf16[256,768]{1,0:T(8,128)(2,1)}, bf16[256,768]{1,0:T(8,128)(2,1)S(1)}, u32[]{:S(2)}) copy-start(bf16[256,768]{1,0:T(8,128)(2,1)S(1)} %fusion.98) | copy-start | bytes 1179652
  106.8 40.4 %copy-start.12 = (bf16[16,768]{1,0:T(8,128)(2,1)S(1)}, bf16[16,768]{1,0:T(8,128)(2,1)}, u32[]{:S(2)}) copy-start(bf16[16,768]{1,0:T(8,128)(2,1)} %get-tuple-element.9) | copy-start | bytes 73732
  122.6 26.9 %copy-start.11 = (bf16[16,768]{1,0:T(8,128)(2,1)S(1)}, bf16[16,768]{1,0:T(8,128)(2,1)}, u32[]{:S(2)}) copy-start(bf16[16,768]{1,0:T(8,128)(2,1)} %get-tuple-element.8) | copy-start | bytes 73732
  122.6 30.1 %copy-start.17 = (bf16[256,768]{1,0:T(8,128)(2,1)S(1)}, bf16[256,768]{1,0:T(8,128)(2,1)}, u32[]{:S(2)}) copy-start(bf16[256,768]{1,0:T(8,128)(2,1)} %copy-done.16) | copy-start | bytes 1179652
  147.2 5.4 %collective-permute-start.5 = (bf16[16,768]{1,0:T(8,128)(2,1)S(1)}, bf16[16,768]{1,0:T(8,128)(2,1)S(1)}, u32[]{:S(2)}, u32[]{:S(2)}) collective-permute-start(bf16[16,768]{1,0:T(8,128)(2,1)S(1)} %copy-done.12), channel_id=1, source_target_pairs={{0,8},{8,16},{16,24},{1,9},{9,17},{17,25},{2,10},{10,18},{18,26},{... | collective-permute-start | bytes 73736 | tf_op jit(solution)/shard_map/ppermute | solution.py:238
  149.4 5.7 %copy-start.2 = (bf16[1,256,1536]{2,1,0:T(8,128)(2,1)S(1)}, bf16[1,256,1536]{2,1,0:T(8,128)(2,1)}, u32[]{:S(2)}) copy-start(bf16[1,256,1536]{2,1,0:T(8,128)(2,1)} %param.10) | copy-start | bytes 2359300
  149.4 5.7 %copy-start.14 = (f32[256]{0:T(256)S(1)}, f32[256]{0:T(256)}, u32[]{:S(2)}) copy-start(f32[256]{0:T(256)} %copy-done.13) | copy-start | bytes 3076
  149.4 5.7 %copy-start.15 = (f32[1536]{0:T(1024)S(1)}, f32[1536]{0:T(1024)}, u32[]{:S(2)}) copy-start(f32[1536]{0:T(1024)} %param.11) | copy-start | bytes 18436
  149.4 5.7 %copy-start.22 = (f32[256,1536]{1,0:T(8,128)S(1)}, f32[256,1536]{1,0:T(8,128)}, u32[]{:S(2)}) copy-start(f32[256,1536]{1,0:T(8,128)} %fusion.15) | copy-start | bytes 4718596
  149.4 5.7 %collective-permute-start.4 = (bf16[16,768]{1,0:T(8,128)(2,1)S(1)}, bf16[16,768]{1,0:T(8,128)(2,1)S(1)}, u32[]{:S(2)}, u32[]{:S(2)}) collective-permute-start(bf16[16,768]{1,0:T(8,128)(2,1)S(1)} %copy-done.11), channel_id=1, source_target_pairs={{8,0},{16,8},{24,16},{9,1},{17,9},{25,17},{10,2},{18,10},{26,18},{... | collective-permute-start | bytes 73736 | tf_op jit(solution)/shard_map/ppermute | solution.py:239
  155.1 3.3 %copy-start.4 = (bf16[256,1536]{1,0:T(8,128)(2,1)S(1)}, bf16[256,1536]{1,0:T(8,128)(2,1)}, u32[]{:S(2)}) copy-start(bf16[256,1536]{1,0:T(8,128)(2,1)} %copy-done.3) | copy-start | bytes 2359300
  155.1 3.3 %copy-start.19 = (f32[256]{0:T(256)S(1)}, f32[256]{0:T(256)}, u32[]{:S(2)}) copy-start(f32[256]{0:T(256)} %get-tuple-element.14) | copy-start | bytes 3076
  (6 other events, 12.2 us)

commit v3 on v2

--- a/solution.py
+++ b/solution.py
@@ -31,28 +31,6 @@
     me, at = place(axis, stride)
     greet(axis, [at(lax.rem(me + step, count)) for step in range(1, count)])
     return me, at
-
-
-def exchange_kernel(axis, stride, count, x_ref, o_ref, local, send_sem, recv_sem):
-    me, at = join(axis, stride, count)
-    copies = []
-    for step in range(1, count):
-        peer = lax.rem(me + step, count)
-        copy = pltpu.make_async_remote_copy(
-            src_ref=x_ref.at[peer],
-            dst_ref=o_ref.at[me],
-            send_sem=send_sem.at[step],
-            recv_sem=recv_sem.at[step],
-            device_id={axis: at(peer)},
-            device_id_type=MESH,
-        )
-        copy.start()
-        copies.append(copy)
-    mine = pltpu.make_async_copy(x_ref.at[me], o_ref.at[me], local)
-    mine.start()
-    mine.wait()
-    for copy in copies:
-        copy.wait()
 
 
 def gather_kernel(axis, stride, count, x_ref, o_ref, local, send_sem, recv_sem):
@@ -124,18 +102,6 @@
     )(x)
 
 
-def exchange(x, axis, cid, stride=1):
-    count = lax.axis_size(axis) // stride
-    return run(
-        functools.partial(exchange_kernel, axis, stride, count),
-        x,
-        jax.ShapeDtypeStruct(x.shape, x.dtype),
-        pltpu.SemaphoreType.DMA,
-        cid,
-        count,
-    )
-
-
 def gather(x, axis, cid, stride=1):
     count = lax.axis_size(axis) // stride
     return run(
@@ -160,34 +126,260 @@
     )
 
 
-def weight_kernel(
-    axis, count, a_ref, g_ref, o_ref, out1, in1, out2, in2, send1, recv1, send2, recv2
+def gelu_slope(argument):
+    return (
+        0.5 * (1.0 + jax.scipy.special.erf(argument * 0.7071067811865476))
+        + argument * jnp.exp(-0.5 * argument * argument) * 0.3989422804014327
+    )
+
+
+def dot(a, b, dims=((1,), (0,))):
+    return lax.dot_general(a, b, (dims, ((), ())), preferred_element_type=F32)
+
+
+ROOT_HALF = 0.7071067811865476
+
+
+def gelu(v):
+    return 0.5 * v * (1.0 + lax.erf(v * ROOT_HALF))
+
+
+def send(src, dst, send_sem, recv_sem, device):
+    copy = pltpu.make_async_remote_copy(
+        src_ref=src,
+        dst_ref=dst,
+        send_sem=send_sem,
+        recv_sem=recv_sem,
+        device_id=device,
+        device_id_type=MESH,
+    )
+    copy.start()
+    return copy
+
+
+def halo_copies(pad, rows, count, sems):
+    me = lax.axis_index("bins")
+    step = DILATION_STEP
+    up = pltpu.make_async_remote_copy(
+        src_ref=pad.at[pl.ds(rows, step)],
+        dst_ref=pad.at[pl.ds(0, step)],
+        send_sem=sems.at[0],
+        recv_sem=sems.at[1],
+        device_id={"bins": lax.rem(me + 1, count)},
+        device_id_type=MESH,
+    )
+    down = pltpu.make_async_remote_copy(
+        src_ref=pad.at[pl.ds(step, step)],
+        dst_ref=pad.at[pl.ds(rows + step, step)],
+        send_sem=sems.at[2],
+        recv_sem=sems.at[3],
+        device_id={"bins": lax.rem(me + count - 1, count)},
+        device_id_type=MESH,
+    )
+    return up, down
+
+
+def halo_start(pad, rows, count, sems):
+    me = lax.axis_index("bins")
+    up, down = halo_copies(pad, rows, count, sems)
+
+    @pl.when(me < count - 1)
+    def _():
+        up.start()
+
+    @pl.when(me > 0)
+    def _():
+        down.start()
+
+    @pl.when(me == 0)
+    def _():
+        pad[0:DILATION_STEP] = jnp.zeros((DILATION_STEP, pad.shape[1]), pad.dtype)
+
+    @pl.when(me == count - 1)
+    def _():
+        pad[rows + DILATION_STEP : rows + 2 * DILATION_STEP] = jnp.zeros(
+            (DILATION_STEP, pad.shape[1]), pad.dtype
+        )
+
+
+def halo_wait(pad, rows, count, sems):
+    me = lax.axis_index("bins")
+    up, down = halo_copies(pad, rows, count, sems)
+
+    @pl.when(me < count - 1)
+    def _():
+        up.wait_send()
+        down.wait_recv()
+
+    @pl.when(me > 0)
+    def _():
+        down.wait_send()
+        up.wait_recv()
+
+
+def meet(groups):
+    barrier = pltpu.get_barrier_semaphore()
+    total = 0
+    for axis, devices in groups:
+        total += len(devices)
+        for device in devices:
+            pl.semaphore_signal(barrier, inc=1, device_id={axis: device}, device_id_type=MESH)
+    pl.semaphore_wait(barrier, total)
+
+
+def front_kernel(
+    count, pairs, f_ref, gain_ref, taps_ref, ow_ref, hits_ref, goal_ref,
+    conv_ref, active_ref, out_ref, all_ref, arrived_ref,
+    pad, picked, held, own, halo_sem, local, send_a, recv_a, send_b, recv_b, send_c, recv_c,
 ):
-    me = lax.axis_index(axis)
+    rows, channels = f_ref.shape
+    hid = ow_ref.shape[0]
+    own_rows = own.shape[0]
+    step = DILATION_STEP
+    me = lax.axis_index("bins")
+    spot, at = place("batch", 2)
+    others = [lax.rem(me + s, count) for s in range(1, count)]
+    peers = [lax.rem(spot + s, pairs) for s in range(1, pairs)]
+    meet([("bins", others), ("batch", [at(p) for p in peers])])
+
+    goals = [
+        send(goal_ref.at[p], arrived_ref.at[spot], send_a.at[i], recv_a.at[i], {"batch": at(p)})
+        for i, p in enumerate(peers)
+    ]
+    mine = pltpu.make_async_copy(goal_ref.at[spot], arrived_ref.at[spot], local)
+    mine.start()
+
+    def norm(i):
+        here = pl.ds(pl.multiple_of(i * step, step), step)
+        wide = f_ref[here, :].astype(F32)
+        inverse = lax.rsqrt(jnp.mean(wide * wide, axis=-1, keepdims=True) + 1e-06)
+        pad[pl.ds(pl.multiple_of(i * step + step, step), step), :] = gelu(
+            wide * inverse * gain_ref[...]
+        ).astype(BF)
+
+    norm(0)
+    norm(rows // step - 1)
+    halo_start(pad, rows, count, halo_sem)
+    pl.loop(1, rows // step - 1)(norm)
+    halo_wait(pad, rows, count, halo_sem)
+
+    @pl.loop(0, hid // 256)
+    def _(i):
+        here = pl.ds(pl.multiple_of(i * 256, 256), 256)
+        total = jnp.zeros((rows, 256), F32)
+        for tap in range(3):
+            total = total + dot(pad[tap * step : tap * step + rows, :], taps_ref[tap, :, here])
+        conv_ref[:, here] = total
+        active_ref[:, here] = gelu(total).astype(BF)
+
+    @pl.loop(0, channels // 256)
+    def _(i):
+        here = pl.ds(pl.multiple_of(i * 256, 256), 256)
+        block = f_ref[:, here].astype(F32) + dot(active_ref[...], ow_ref[:, here])
+        block = block.astype(BF)
+        out_ref[:, here] = block
+        rows_of = dot(hits_ref[...], block).astype(BF)
+        for j in range(count):
+            picked[j, :, here] = rows_of[j * own_rows : (j + 1) * own_rows]
+
+    legs = [
+        send(picked.at[p], held.at[i], send_b.at[i], recv_b.at[i], {"bins": p})
+        for i, p in enumerate(others)
+    ]
+    total = picked[me].astype(F32)
+    for i, leg in enumerate(legs):
+        leg.wait_recv()
+        total = total + held[i].astype(F32)
+    own[...] = total.astype(BF)
+    spread = [
+        send(own, all_ref.at[spot], send_c.at[i], recv_c.at[i], {"batch": at(p)})
+        for i, p in enumerate(peers)
+    ]
+    all_ref[spot] = own[...]
+    mine.wait()
+    for leg in legs:
+        leg.wait_send()
+    for copy in goals + spread:
+        copy.wait()
+
+
+def front(features, gain, taps, out_weight, hits, goals):
+    count = lax.axis_size("bins")
+    pairs = goals.shape[0]
+    rows, channels = features.shape
+    hid = out_weight.shape[0]
+    own_rows = hits.shape[0] // count
+    dma = pltpu.SemaphoreType.DMA
+    return pl.pallas_call(
+        functools.partial(front_kernel, count, pairs),
+        out_shape=(
+            jax.ShapeDtypeStruct((rows, hid), F32),
+            jax.ShapeDtypeStruct((rows, hid), BF),
+            jax.ShapeDtypeStruct((rows, channels), BF),
+            jax.ShapeDtypeStruct((pairs, own_rows, channels), BF),
+            jax.ShapeDtypeStruct(goals.shape, F32),
+        ),
+        in_specs=[vmem()] * 6,
+        out_specs=(vmem(),) * 5,
+        scratch_shapes=[
+            pltpu.VMEM((rows + 2 * DILATION_STEP, channels), BF),
+            pltpu.VMEM((count, own_rows, channels), BF),
+            pltpu.VMEM((count, own_rows, channels), BF),
+            pltpu.VMEM((own_rows, channels), BF),
+            dma((4,)),
+            dma,
+            dma((pairs,)),
+            dma((pairs,)),
+            dma((count,)),
+            dma((count,)),
+            dma((pairs,)),
+            dma((pairs,)),
+        ],
+        compiler_params=pltpu.CompilerParams(
+            collective_id=1, has_side_effects=True, vmem_limit_bytes=48 * 1024 * 1024
+        ),
+    )(features, gain.reshape(1, channels), taps, out_weight, hits, goals)
+
+
+def tail_kernel(
+    count, batch, f_ref, gain_ref, taps_ref, ow_ref, conv_ref, a_ref, g_ref, parts_ref,
+    ig_ref, og_ref,
+    pad, hidden_grad, out1, in1, out2, in2, bsum, held, osum,
+    halo_sem, send1, recv1, send2, recv2, send3, recv3, send4, recv4,
+):
+    rows, channels = f_ref.shape
+    hid = ow_ref.shape[0]
+    high = osum.shape[0]
+    step_rows = DILATION_STEP
+    me = lax.axis_index("bins")
+    seq = lax.axis_index("batch")
+    others = [lax.rem(me + s, count) for s in range(1, count)]
+    peers = [lax.rem(seq + s, batch) for s in range(1, batch)]
+    meet([("bins", others), ("batch", peers)])
     half = count // 2
     spot, parity = lax.div(me, 2), lax.rem(me, 2)
     buddy = 2 * spot + 1 - parity
     quarters = [lax.rem(spot + step, half) for step in range(half)]
-    greet(axis, [buddy] + [2 * quarters[step] + parity for step in range(1, half)])
+    order = list(range(1, half)) + [0]
 
     def term(part):
-        return lax.dot_general(
-            a_ref[...], g_ref[part], (((0,), (0,)), ((), ())), preferred_element_type=F32
-        )
-
-    order = list(range(1, half)) + [0]
+        return dot(a_ref[...], parts_ref[part], ((0,), (0,)))
+
     first = {}
     for step in order:
         out1[step] = term(2 * quarters[step] + 1 - parity).astype(BF)
-        first[step] = pltpu.make_async_remote_copy(
-            src_ref=out1.at[step],
-            dst_ref=in1.at[step],
-            send_sem=send1.at[step],
-            recv_sem=recv1.at[step],
-            device_id={axis: buddy},
-            device_id_type=MESH,
+        first[step] = send(
+            out1.at[step], in1.at[step], send1.at[step], recv1.at[step], {"bins": buddy}
         )
-        first[step].start()
+
+    @pl.loop(0, hid // 256)
+    def _(i):
+        here = pl.ds(pl.multiple_of(i * 256, 256), 256)
+        grad = dot(g_ref[...], ow_ref[here, :], ((1,), (1,))) * gelu_slope(conv_ref[:, here])
+        pad[step_rows : step_rows + rows, here] = grad.astype(BF)
+
+    halo_start(pad, rows, count, halo_sem)
+
     second = {}
     for step in order:
         total = term(2 * quarters[step] + parity)
@@ -195,60 +387,106 @@
         total = total + in1[step].astype(F32)
         if step:
             out2[step] = total.astype(BF)
-            second[step] = pltpu.make_async_remote_copy(
-                src_ref=out2.at[step],
-                dst_ref=in2.at[step],
-                send_sem=send2.at[step],
-                recv_sem=recv2.at[step],
-                device_id={axis: 2 * quarters[step] + parity},
-                device_id_type=MESH,
+            second[step] = send(
+                out2.at[step],
+                in2.at[step],
+                send2.at[step],
+                recv2.at[step],
+                {"bins": 2 * quarters[step] + parity},
             )
-            second[step].start()
+        else:
+            out2[0] = total.astype(BF)
+
+    halo_wait(pad, rows, count, halo_sem)
+
+    @pl.loop(0, channels // 256)
+    def _(i):
+        here = pl.ds(pl.multiple_of(i * 256, 256), 256)
+        total = jnp.zeros((rows, 256), F32)
+        for tap in range(3):
+            shift = (2 - tap) * step_rows
+            total = total + dot(
+                pad[shift : shift + rows, :], taps_ref[tap, here, :], ((1,), (1,))
+            )
+        hidden_grad[:, here] = total
+
+    @pl.loop(0, rows // step_rows)
+    def _(i):
+        here = pl.ds(pl.multiple_of(i * step_rows, step_rows), step_rows)
+        wide = f_ref[here, :].astype(F32)
+        inverse = lax.rsqrt(jnp.mean(wide * wide, axis=-1, keepdims=True) + 1e-06)
+        gain = gain_ref[...]
+        normed_grad = hidden_grad[here, :] * gelu_slope(wide * inverse * gain) * gain
+        back = inverse * normed_grad - wide * (inverse * inverse * inverse) * jnp.mean(
+            normed_grad * wide, axis=-1, keepdims=True
+        )
+        ig_ref[here, :] = (g_ref[here, :].astype(F32) + back).astype(BF)
+
     for step in range(1, half):
         second[step].wait_recv()
-        total = total + in2[step].astype(F32)
-    o_ref[...] = total.astype(o_ref.dtype)
+    for j in range(batch):
+        part = out2[0, j * high : (j + 1) * high].astype(F32)
+        for step in range(1, half):
+            part = part + in2[step, j * high : (j + 1) * high].astype(F32)
+        bsum[j] = part.astype(BF)
+    third = [
+        send(bsum.at[p], held.at[i], send3.at[i], recv3.at[i], {"batch": p})
+        for i, p in enumerate(peers)
+    ]
+    total = bsum[seq].astype(F32)
+    for i, copy in enumerate(third):
+        copy.wait_recv()
+        total = total + held[i].astype(F32)
+    osum[...] = total.astype(BF)
+    fourth = [
+        send(osum, og_ref.at[me], send4.at[i], recv4.at[i], {"bins": p})
+        for i, p in enumerate(others)
+    ]
+    og_ref[me] = osum[...]
     for step in range(half):
         first[step].wait_send()
     for step in range(1, half):
         second[step].wait_send()
-
-
-def weight_sum(active, grad, axis, cid):
-    count, rows, wide = grad.shape
+    for copy in third:
+        copy.wait_send()
+    for copy in fourth:
+        copy.wait()
+
+
+def tail(features, gain, taps, out_weight, conv_sum, active, grad, parts):
+    count, rows, wide = parts.shape
+    batch = lax.axis_size("batch")
+    channels = features.shape[1]
     hid = active.shape[1]
     half = count // 2
+    high = hid // batch
+    dma = pltpu.SemaphoreType.DMA
     return pl.pallas_call(
-        functools.partial(weight_kernel, axis, count),
-        out_shape=jax.ShapeDtypeStruct((hid, wide), BF),
-        in_specs=[vmem(), vmem()],
-        out_specs=vmem(),
-        scratch_shapes=[pltpu.VMEM((half, hid, wide), BF) for _ in range(4)]
-        + [pltpu.SemaphoreType.DMA((half,)) for _ in range(4)],
+        functools.partial(tail_kernel, count, batch),
+        out_shape=(
+            jax.ShapeDtypeStruct((rows, channels), BF),
+            jax.ShapeDtypeStruct((count, high, wide), BF),
+        ),
+        in_specs=[vmem()] * 8,
+        out_specs=(vmem(),) * 2,
+        scratch_shapes=[
+            pltpu.VMEM((rows + 2 * DILATION_STEP, hid), BF),
+            pltpu.VMEM((rows, channels), F32),
+        ]
+        + [pltpu.VMEM((half, hid, wide), BF) for _ in range(4)]
+        + [
+            pltpu.VMEM((batch, high, wide), BF),
+            pltpu.VMEM((batch, high, wide), BF),
+            pltpu.VMEM((high, wide), BF),
+            dma((4,)),
+        ]
+        + [dma((half,)) for _ in range(4)]
+        + [dma((batch,)) for _ in range(2)]
+        + [dma((count,)) for _ in range(2)],
         compiler_params=pltpu.CompilerParams(
-            collective_id=cid, has_side_effects=True, vmem_limit_bytes=32 * 1024 * 1024
+            collective_id=6, has_side_effects=True, vmem_limit_bytes=56 * 1024 * 1024
         ),
-    )(active, grad)
-
-
-def with_halo(block, axis, width):
-    count = lax.axis_size(axis)
-    forward = [(i, i + 1) for i in range(count - 1)]
-    backward = [(target, source) for source, target in forward]
-    low = lax.ppermute(block[-width:], axis, forward)
-    high = lax.ppermute(block[:width], axis, backward)
-    return jnp.concatenate([low, block, high], axis=0)
-
-
-def gelu_slope(argument):
-    return (
-        0.5 * (1.0 + jax.scipy.special.erf(argument * 0.7071067811865476))
-        + argument * jnp.exp(-0.5 * argument * argument) * 0.3989422804014327
-    )
-
-
-def dot(a, b, dims=((1,), (0,))):
-    return lax.dot_general(a, b, (dims, ((), ())), preferred_element_type=F32)
+    )(features, gain.reshape(1, channels), taps, out_weight, conv_sum, active, grad, parts)
 
 
 def per_device(
@@ -289,35 +527,20 @@
     pieces = jnp.where(odd == 1, pieces[:, :, ::-1], pieces)
     pieces = pieces.reshape(own_genes, pairs, 2 * part).transpose(1, 0, 2)
     counted = jnp.broadcast_to(own_count.astype(F32)[None, :, None], (pairs, own_genes, 128))
-    arrived = exchange(jnp.concatenate([pieces, counted], axis=2), "batch", 1, 2)
-    track_target = arrived[:, :, : 2 * part]
-    track_count = arrived[:, :, 2 * part : 2 * part + 1].astype(jnp.int32)
-
-    widened = features[0].astype(F32)
-    inverse = lax.rsqrt(jnp.mean(widened * widened, axis=-1, keepdims=True) + 1e-06)
-    normed = widened * inverse * norm_gain
-    hidden = jax.nn.gelu(normed, approximate=False).astype(BF)
-    padded = with_halo(hidden, "bins", DILATION_STEP)
-    conv_sum = jnp.zeros((rows, hid), F32)
-    for tap in range(3):
-        conv_sum = conv_sum + dot(
-            padded[tap * DILATION_STEP : tap * DILATION_STEP + rows], taps[tap]
-        )
-    active = jax.nn.gelu(conv_sum, approximate=False).astype(BF)
-    block_out = (widened + dot(active, out_weight)).astype(BF)
-
     positions = bin_index * rows + jnp.arange(rows, dtype=jnp.int32)
     listed = jnp.arange(exons, dtype=jnp.int32)[None, :] < exon_count[0][:, None]
     hits = (
         (exon_bins[0][:, :, None] == positions[None, None, :]) & listed[:, :, None]
     ).reshape(genes * exons, rows).astype(BF)
-    picked = dot(hits, block_out).astype(BF).reshape(bin_devices, own_rows, channels)
-    own_picked = reduce_pieces(picked, "bins", 2)
-    own_picked, block_out = lax.optimization_barrier((own_picked, block_out))
+    conv_sum, active, block_out, all_picked, arrived = front(
+        features[0], norm_gain, taps, out_weight, hits, jnp.concatenate([pieces, counted], axis=2)
+    )
+    track_target = arrived[:, :, : 2 * part]
+    track_count = arrived[:, :, 2 * part : 2 * part + 1].astype(jnp.int32)
     partner = lax.ppermute(
         block_out, "bins", [(i, bin_devices - 1 - i) for i in range(bin_devices)]
     )
-    all_picked = gather(own_picked, "batch", 3, 2).reshape(pairs * own_rows, channels)
+    all_picked = all_picked.reshape(pairs * own_rows, channels)
 
     logits = jnp.concatenate([dot(all_picked, head_weight), dot(all_picked, other_head)], axis=1)
     logits = logits.reshape(pairs, own_genes, exons, 2 * part)
@@ -348,30 +571,19 @@
     rc_grad = block_out.astype(F32) - 0.5 * dot(mirrored, both_maps)
     block_grad = (head_back + rc_grad).astype(BF)
 
-    act_grad = (dot(block_grad, out_weight, ((1,), (1,))) * gelu_slope(conv_sum)).astype(BF)
-    padded_grad = with_halo(act_grad, "bins", DILATION_STEP)
-
     wide = channels // bin_devices
-    bins_sum = weight_sum(
-        active, block_grad.reshape(rows, bin_devices, wide).transpose(1, 0, 2), "bins", 6
-    )
-    own_sum = reduce_pieces(
-        bins_sum.reshape(batch_devices, hid // batch_devices, wide), "batch", 7
-    )
-    out_weight_grad = gather(own_sum, "bins", 8).transpose(1, 0, 2)
-    out_weight_grad = out_weight_grad.reshape(hid // batch_devices, channels).astype(F32)
-
-    hidden_grad = jnp.zeros((rows, channels), F32)
-    for tap in range(3):
-        shift = (2 - tap) * DILATION_STEP
-        hidden_grad = hidden_grad + dot(
-            padded_grad[shift : shift + rows], taps[tap], ((1,), (1,))
-        )
-    normed_grad = hidden_grad * gelu_slope(normed) * norm_gain
-    norm_back = inverse * normed_grad - widened * inverse**3 * jnp.mean(
-        normed_grad * widened, axis=-1, keepdims=True
-    )
-    input_grad = (block_grad.astype(F32) + norm_back).astype(BF)
+    input_grad, own_parts = tail(
+        features[0],
+        norm_gain,
+        taps,
+        out_weight,
+        conv_sum,
+        active,
+        block_grad,
+        block_grad.reshape(rows, bin_devices, wide).transpose(1, 0, 2),
+    )
+    out_weight_grad = own_parts.transpose(1, 0, 2).reshape(hid // batch_devices, channels)
+    out_weight_grad = out_weight_grad.astype(F32)
     return (input_grad[None], out_weight_grad)
 
 

time: 161 us -> 138 us (0.86)
  matrix products: 43.5 us -> 11.1 us
  waiting for transfers between devices: 0.02 us -> 17.3 us
  starting transfers between devices: 9.31 us -> 0.42 us
  other arithmetic: 12.3 us -> 3.87 us
  Pallas kernels: 84.7 us -> 92.9 us
  local copies, waits for them, and re-layouts: 8.75 us -> 10.8 us
    pallas_call x1 -> x2, Pallas kernels: 15.8 us -> 73.9 us  [the longest x1 44.9 us: tail(): pl.pallas_call(functools.partial(tail_kernel, count, batch), out_shape=(j...]
    pallas_call x7 -> x2, Pallas kernels: 68.9 us -> 19 us  [run(): pl.pallas_call(kernel, out_shape=out, in_specs=[vmem()], out_specs=vmem()...]
    dot_general x15 -> x6, matrix products: 43.5 us -> 11.1 us  [dot(): return lax.dot_general(a, b, (dims, ((), ())), preferred_element_type=F32)]
    ppermute x1, waiting for transfers between devices: 0.01 us -> 17.3 us  [per_device(): lax.ppermute(block_out, 'bins', [(i, bin_devices - 1 - i) for i in range(...]
    ppermute x4 -> x0, starting transfers between devices: 8.92 us -> none  [the longest x2 6.35 us: with_halo(): high = lax.ppermute(block[:width], axis, backward)]
    convert_element_type x1, other arithmetic: 4.84 us -> 0.1 us  [per_device(): hits = ((exon_bins[0][:, :, None] == positions[None, None, :]) & listed[:...]
    unnamed x49 -> x26, local copies, waits for them, and re-layouts: 1.63 us -> 4.96 us
  transfers between devices with their start and end apart: 6 -> 2, of which waited for: 0 -> 1; matrix products, arithmetic and copies ran while one was open for 22% -> 9% of each run, Pallas kernels for 16% -> 21%
where the time goes in v3:
time: 138 us; the launch traced here: 137 us
  Pallas kernels  92.9 us (67%)
  waiting for transfers between devices  17.3 us (13%)
  matrix products  11.1 us (8%)
  local copies, waits for them, and re-layouts  10.8 us (8%)
  other arithmetic  3.87 us (3%)
    pallas_call x1, Pallas kernels, tail(): pl.pallas_call(functools.partial(tail_kernel, count, batch), out_shape=(j...  44.9 us
    pallas_call x1, Pallas kernels, front(): pl.pallas_call(functools.partial(front_kernel, count, pairs), out_shape=(...  29 us
    pallas_call x2, Pallas kernels, run(): pl.pallas_call(kernel, out_shape=out, in_specs=[vmem()], out_specs=vmem()...  19 us
    ppermute x1, waiting for transfers between devices, per_device(): lax.ppermute(block_out, 'bins', [(i, bin_devices - 1 - i) for i in range(...  17.3 us
    dot_general x6, matrix products, dot(): return lax.dot_general(a, b, (dims, ((), ())), preferred_element_type=F32)  11.1 us
    unnamed x26, local copies, waits for them, and re-layouts  4.96 us
  transfers between devices with their start and end apart: 2, of which 1 were waited for; matrix products, arithmetic and copies ran while one was open for 9% of the time, Pallas kernels for 21%

profile of v3, /device:TPU:15, one launch (start us, length us, event | category | flops | bytes accessed | tf_op | source)
XLA Modules:
  0.0 137.5 jit_solution(14427924723156499611)
XLA Ops:
  1.0 1.0 fusion.21
  2.0 0.8 fusion.22
  2.8 0.9 squeeze.13
  4.0 0.7 compare_bitcast_fusion
  5.1 0.8 copy.16
  6.0 0.7 iota_compare_fusion.6
  7.3 1.7 %copy-done = bf16[768,1536]{1,0:T(8,128)(2,1)S(1)} copy-done((bf16[768,1536]{1,0:T(8,128)(2,1)S(1)}, bf16[768,1536]{1,0:T(8,128)(2,1)}, u32[]{:S(2)}) %copy-start) | copy-done | bytes 2359320
  8.9 29.0 %shard_map.113 = (f32[256,768]{1,0:T(8,128)S(1)}, bf16[256,768]{1,0:T(8,128)(2,1)S(1)}, bf16[256,1536]{1,0:T(8,128)(2,1)S(1)}, bf16[4,32,1536]{2,1,0:T(8,128)(2,1)S(1)}, f32[4,4,1152]{2,1,0:T(4,128)S(1)}) custom-call(bf16[256,1536]{1,0:T(8,128)(2,1)S(1)} %bitcast.40, f32[1,1536]{1,0:T(1,128)S(1)} %reshape.124.gain_ref, bf16[3,1536,768]{2,1,0:T(8,128)(2,1)} %taps_ref.3, ...), custom_call_target="tpu_custom_call" | custom-call | tf_op jit(solution)/shard_map/pallas_call | solution.py:313
  37.9 0.9 copy-done.2
  38.8 0.7 copy-done.3
  40.0 1.8 %fusion.23 = f32[128,512]{1,0:T(8,128)S(1)} fusion(bf16[128,1536]{1,0:T(8,128)(2,1)S(1)} %bitcast.43, bf16[1536,512]{1,0:T(8,128)(2,1)} %param.14), kind=kOutput, calls=%fused_computation.52 | convolution fusion | flops 201326592 | bytes 2228224 | tf_op jit(solution)/shard_map/dot_general | solution.py:137
  41.7 17.3 %collective-permute-done.1 = bf16[256,1536]{1,0:T(8,128)(2,1)S(1)} collective-permute-done((bf16[256,1536]{1,0:T(8,128)(2,1)S(1)}, bf16[256,1536]{1,0:T(8,128)(2,1)S(1)}, u32[]{:S(2)}, u32[]{:S(2)}) %collective-permute-start.1) | collective-permute-done | bytes 786464 | tf_op jit(solution)/shard_map/ppermute | solution.py:540
  59.1 4.2 %fusion.4 = f32[256,1536]{1,0:T(8,128)} fusion(s32[1536]{0:T(1024)S(1)} %copy-done.11, bf16[256,1536]{1,0:T(8,128)(2,1)S(1)} %get-tuple-element.13, bf16[256,1536]{1,0:T(8,128)(2,1)S(1)} %collective-permute-done.1, s32[256]{0:T(256)S(1)} %iota_subtract_fusion), kind=kOutput, calls=%fused_computation.8 | convolution fusion | flops 1425080320 | bytes 3152896 | tf_op jit(solution)/shard_map/dot_general | solution.py:137
  63.3 1.9 %fusion.24 = f32[128,512]{1,0:T(8,128)S(1)} fusion(bf16[128,1536]{1,0:T(8,128)(2,1)S(1)} %bitcast.44, bf16[1536,512]{1,0:T(8,128)(2,1)} %collective-permute-done), kind=kOutput, calls=%fused_computation.53 | convolution fusion | flops 201326592 | bytes 2228224 | tf_op jit(solution)/shard_map/dot_general | solution.py:137
  65.8 0.6 fusion.11
  66.5 2.2 %fusion.6 = bf16[128,1536]{1,0:T(8,128)(2,1)S(1)} fusion(f32[128,1536]{1,0:T(8,128)S(1)} %fusion.11, bf16[1536,512]{1,0:T(8,128)(2,1)} %collective-permute-done, bf16[128,1024]{1,0:T(8,128)(2,1)S(1)} %fusion.9), kind=kOutput, calls=%fused_computation.12 | convolution fusion | flops 201719808 | bytes 2883584 | tf_op jit(solution)/shard_map/dot_general | solution.py:137
  68.7 11.6 %shard_map.114.x_ref = bf16[32,1536]{1,0:T(8,128)(2,1)S(1)} custom-call(bf16[4,32,1536]{2,1,0:T(8,128)(2,1)S(1)} %bitcast.42), custom_call_target="tpu_custom_call" | custom-call | tf_op jit(solution)/shard_map/pallas_call | solution.py:87
  80.3 7.4 %shard_map.115 = bf16[4,32,1536]{2,1,0:T(8,128)(2,1)S(1)} custom-call(bf16[32,1536]{1,0:T(8,128)(2,1)S(1)} %shard_map.114.x_ref), custom_call_target="tpu_custom_call" | custom-call | tf_op jit(solution)/shard_map/pallas_call | solution.py:87
  87.7 0.5 fusion.5.g_ref
  88.5 1.2 copy.21
  89.7 44.9 %shard_map.116 = (bf16[256,1536]{1,0:T(8,128)(2,1)}, bf16[4,96,384]{2,1,0:T(8,128)(2,1)}) custom-call(bf16[256,1536]{1,0:T(8,128)(2,1)} %bitcast.39, f32[1,1536]{1,0:T(1,128)} %copy-done.4, bf16[3,1536,768]{2,1,0:T(8,128)(2,1)} %taps_ref.3, bf16[768,1536]{1,0:T(8,128)(2,1)} %ow_ref.3, f32[256,768]{1,0:T(8,128)} %copy-done.2, bf16[256,768]{1,0:T(8,128)(2,1)} %copy-done.3, ...), custom_call_target="tpu_custom_call" | custom-call | tf_op jit(solution)/shard_map/pallas_call | solution.py:464
  134.6 1.1 convert_bitcast_fusion
  135.7 0.9 copy.23
  136.6 0.9 copy.28
  (49 shorter events, 2.9 us)
Async XLA Ops:
  0.6 6.3 %copy-start.10 = (s32[1,16]{1,0:T(1,128)S(1)}, s32[1,16]{1,0:T(1,128)}, u32[]{:S(2)}) copy-start(s32[1,16]{1,0:T(1,128)} %param.17) | copy-start | bytes 196
  0.6 6.5 %copy-start.9 = (f32[1536]{0:T(1024)S(1)}, f32[1536]{0:T(1024)}, u32[]{:S(2)}) copy-start(f32[1536]{0:T(1024)} %param.11) | copy-start | bytes 18436
  0.7 6.6 %copy-start.1 = (bf16[1,256,1536]{2,1,0:T(8,128)(2,1)S(1)}, bf16[1,256,1536]{2,1,0:T(8,128)(2,1)}, u32[]{:S(2)}) copy-start(bf16[1,256,1536]{2,1,0:T(8,128)(2,1)} %param.10) | copy-start | bytes 2359300
  0.7 62.6 %collective-permute-start = (bf16[1536,512]{1,0:T(8,128)(2,1)}, bf16[1536,512]{1,0:T(8,128)(2,1)}, u32[]{:S(2)}, u32[]{:S(2)}) collective-permute-start(bf16[1536,512]{1,0:T(8,128)(2,1)} %param.14), channel_id=1, source_target_pairs={{0,1},{1,0},{2,3},{3,2},{4,5},{5,4},{6,7},{7,6},{8,9},{9,8},{10,11... | collective-permute-start | bytes 4718600 | tf_op jit(solution)/shard_map/ppermute | solution.py:515
  7.1 30.8 %copy-start.4 = (f32[1,1536]{1,0:T(1,128)}, f32[1,1536]{1,0:T(1,128)S(1)}, u32[]{:S(2)}) copy-start(f32[1,1536]{1,0:T(1,128)S(1)} %reshape.124.gain_ref) | copy-start | bytes 18436
  7.3 1.7 %copy-start = (bf16[768,1536]{1,0:T(8,128)(2,1)S(1)}, bf16[768,1536]{1,0:T(8,128)(2,1)}, u32[]{:S(2)}) copy-start(bf16[768,1536]{1,0:T(8,128)(2,1)} %ow_ref.3) | copy-start | bytes 7077892
  37.9 0.9 copy-start.2
  38.8 0.7 copy-start.3
  39.5 19.6 %copy-start.11 = (s32[1536]{0:T(1024)S(1)}, s32[1536]{0:T(1024)}, u32[]{:S(2)}) copy-start(s32[1536]{0:T(1024)} %param.15) | copy-start | bytes 18436
  39.5 19.5 %collective-permute-start.1 = (bf16[256,1536]{1,0:T(8,128)(2,1)S(1)}, bf16[256,1536]{1,0:T(8,128)(2,1)S(1)}, u32[]{:S(2)}, u32[]{:S(2)}) collective-permute-start(bf16[256,1536]{1,0:T(8,128)(2,1)S(1)} %get-tuple-element.13), channel_id=1, source_target_pairs={{0,24},{8,16},{16,8},{24,0},{1,25},{9,17},{17,9},{25,1},{2,26},{10... | collective-permute-start | bytes 2359304 | tf_op jit(solution)/shard_map/ppermute | solution.py:540
  63.3 2.6 %copy-start.6 = (bf16[1536,512]{1,0:T(8,128)(2,1)S(1)}, bf16[1536,512]{1,0:T(8,128)(2,1)}, u32[]{:S(2)}) copy-start(bf16[1536,512]{1,0:T(8,128)(2,1)} %param.14) | copy-start | bytes 4718596
  66.5 21.3 %copy-start.7 = (f32[256,1536]{1,0:T(8,128)S(1)}, f32[256,1536]{1,0:T(8,128)}, u32[]{:S(2)}) copy-start(f32[256,1536]{1,0:T(8,128)} %fusion.4) | copy-start | bytes 4718596
  88.2 1.5 %copy-start.5 = (bf16[256,1536]{1,0:T(8,128)(2,1)}, bf16[256,1536]{1,0:T(8,128)(2,1)S(1)}, u32[]{:S(2)}) copy-start(bf16[256,1536]{1,0:T(8,128)(2,1)S(1)} %fusion.5.g_ref) | copy-start | bytes 2359300
  134.6 2.0 %copy-start.8 = (bf16[256,1536]{1,0:T(8,128)(2,1)S(1)}, bf16[256,1536]{1,0:T(8,128)(2,1)}, u32[]{:S(2)}) copy-start(bf16[256,1536]{1,0:T(8,128)(2,1)} %get-tuple-element.14) | copy-start | bytes 2359300

commit v4 on v3

--- a/solution.py
+++ b/solution.py
@@ -20,110 +20,8 @@
     return me, lambda at: at * stride + rest
 
 
-def greet(axis, devices):
-    barrier = pltpu.get_barrier_semaphore()
-    for device in devices:
-        pl.semaphore_signal(barrier, inc=1, device_id={axis: device}, device_id_type=MESH)
-    pl.semaphore_wait(barrier, len(devices))
-
-
-def join(axis, stride, count):
-    me, at = place(axis, stride)
-    greet(axis, [at(lax.rem(me + step, count)) for step in range(1, count)])
-    return me, at
-
-
-def gather_kernel(axis, stride, count, x_ref, o_ref, local, send_sem, recv_sem):
-    me, at = join(axis, stride, count)
-    copies = []
-    for step in range(1, count):
-        peer = lax.rem(me + step, count)
-        copy = pltpu.make_async_remote_copy(
-            src_ref=x_ref,
-            dst_ref=o_ref.at[me],
-            send_sem=send_sem.at[step],
-            recv_sem=recv_sem.at[step],
-            device_id={axis: at(peer)},
-            device_id_type=MESH,
-        )
-        copy.start()
-        copies.append(copy)
-    mine = pltpu.make_async_copy(x_ref, o_ref.at[me], local)
-    mine.start()
-    mine.wait()
-    for copy in copies:
-        copy.wait()
-
-
-def reduce_kernel(axis, stride, count, x_ref, o_ref, held, send_sem, recv_sem):
-    me, at = join(axis, stride, count)
-    copies = []
-    for step in range(1, count):
-        peer = lax.rem(me + step, count)
-        copy = pltpu.make_async_remote_copy(
-            src_ref=x_ref.at[peer],
-            dst_ref=held.at[step],
-            send_sem=send_sem.at[step],
-            recv_sem=recv_sem.at[step],
-            device_id={axis: at(peer)},
-            device_id_type=MESH,
-        )
-        copy.start()
-        copies.append(copy)
-    total = x_ref[me].astype(F32)
-    for step in range(1, count):
-        copies[step - 1].wait_recv()
-        total = total + held[step].astype(F32)
-    o_ref[...] = total.astype(o_ref.dtype)
-    for copy in copies:
-        copy.wait_send()
-
-
 def vmem():
     return pl.BlockSpec(memory_space=pltpu.VMEM)
-
-
-def run(kernel, x, out, scratch, collective_id, count):
-    return pl.pallas_call(
-        kernel,
-        out_shape=out,
-        in_specs=[vmem()],
-        out_specs=vmem(),
-        scratch_shapes=[
-            scratch,
-            pltpu.SemaphoreType.DMA((count,)),
-            pltpu.SemaphoreType.DMA((count,)),
-        ],
-        compiler_params=pltpu.CompilerParams(
-            collective_id=collective_id,
-            has_side_effects=True,
-            vmem_limit_bytes=32 * 1024 * 1024,
-        ),
-    )(x)
-
-
-def gather(x, axis, cid, stride=1):
-    count = lax.axis_size(axis) // stride
-    return run(
-        functools.partial(gather_kernel, axis, stride, count),
-        x,
-        jax.ShapeDtypeStruct((count,) + x.shape, x.dtype),
-        pltpu.SemaphoreType.DMA,
-        cid,
-        count,
-    )
-
-
-def reduce_pieces(x, axis, cid, stride=1):
-    count = lax.axis_size(axis) // stride
-    return run(
-        functools.partial(reduce_kernel, axis, stride, count),
-        x,
-        jax.ShapeDtypeStruct(x.shape[1:], x.dtype),
-        pltpu.VMEM(x.shape, x.dtype),
-        cid,
-        count,
-    )
 
 
 def gelu_slope(argument):
@@ -489,6 +387,132 @@
     )(features, gain.reshape(1, channels), taps, out_weight, conv_sum, active, grad, parts)
 
 
+def middle_kernel(
+    count, pairs, out_ref, all_ref, head_ref, other_ref, goal_ref, sums_ref, hits_ref,
+    perm_row_ref, perm_col_ref,
+    bg_ref, parts_ref,
+    partner, maps, rowgrad, pieces, held, own, seq, mirrored,
+    send_m, recv_m, send_a, recv_a, send_b, recv_b,
+):
+    rows, channels = out_ref.shape
+    part = head_ref.shape[1]
+    own_rows = own.shape[0]
+    wide = parts_ref.shape[2]
+    me = lax.axis_index("bins")
+    spot, at = place("batch", 2)
+    others = [lax.rem(me + s, count) for s in range(1, count)]
+    peers = [lax.rem(spot + s, pairs) for s in range(1, pairs)]
+    meet([("bins", others), ("batch", [at(p) for p in peers])])
+
+    mirror = send(out_ref, partner, send_m, recv_m, {"bins": count - 1 - me})
+
+    picked = all_ref[...].reshape(pairs * own_rows, channels)
+    for side, weight in enumerate((head_ref, other_ref)):
+        logits = dot(picked, weight[...])
+        predicted = jnp.maximum(logits, 0.0) + jnp.log1p(jnp.exp(-jnp.abs(logits)))
+        covered = dot(sums_ref[...], predicted.astype(BF))
+        goal = goal_ref[:, side * part : (side + 1) * part]
+        spread = (1.0 - goal / (1.0 + covered)).astype(BF)
+        back = dot(sums_ref[...], spread, ((0,), (0,)))
+        rowgrad[side] = (back * jax.nn.sigmoid(logits)).astype(BF)
+
+    @pl.loop(0, channels // 256)
+    def _(i):
+        here = pl.ds(pl.multiple_of(i * 256, 256), 256)
+        grad = dot(rowgrad[0], head_ref[here, :], ((1,), (1,)))
+        grad = (grad + dot(rowgrad[1], other_ref[here, :], ((1,), (1,)))).astype(BF)
+        for j in range(pairs):
+            pieces[j, :, here] = grad[j * own_rows : (j + 1) * own_rows]
+
+    legs = [
+        send(pieces.at[p], held.at[i], send_a.at[i], recv_a.at[i], {"batch": at(p)})
+        for i, p in enumerate(peers)
+    ]
+
+    @pl.loop(0, channels // 256)
+    def _(i):
+        here = pl.ds(pl.multiple_of(i * 256, 256), 256)
+        down = lax.broadcasted_iota(jnp.int32, (channels, 256), 0)
+        along = lax.broadcasted_iota(jnp.int32, (channels, 256), 1) + i * 256
+        first = jnp.where(down == perm_row_ref[:, here], 1.0, 0.0)
+        second = jnp.where(along == perm_col_ref[...], 1.0, 0.0)
+        maps[:, here] = (first + second).astype(BF)
+
+    total = pieces[spot].astype(F32)
+    for i, leg in enumerate(legs):
+        leg.wait_recv()
+        total = total + held[i].astype(F32)
+    own[...] = total.astype(BF)
+    spread_out = [
+        send(own, seq.at[me], send_b.at[i], recv_b.at[i], {"bins": p})
+        for i, p in enumerate(others)
+    ]
+    seq[me] = own[...]
+
+    mirror.wait()
+    flip = jnp.where(
+        lax.broadcasted_iota(jnp.int32, (rows, rows), 0)
+        + lax.broadcasted_iota(jnp.int32, (rows, rows), 1)
+        == rows - 1,
+        1.0,
+        0.0,
+    ).astype(BF)
+    mirrored[...] = dot(flip, partner[...]).astype(BF)
+    for copy in spread_out:
+        copy.wait()
+
+    @pl.loop(0, channels // 256)
+    def _(i):
+        here = pl.ds(pl.multiple_of(i * 256, 256), 256)
+        grads = seq[:, :, here].reshape(count * own_rows, 256)
+        block = dot(hits_ref[...], grads, ((0,), (0,))) + out_ref[:, here].astype(F32)
+        bg_ref[:, here] = (block - 0.5 * dot(mirrored[...], maps[:, here])).astype(BF)
+
+    for j in range(count):
+        parts_ref[j] = bg_ref[:, j * wide : (j + 1) * wide]
+    for leg in legs:
+        leg.wait_send()
+
+
+def middle(block_out, all_picked, head, other, goals, sums, hits, perm):
+    count = lax.axis_size("bins")
+    pairs, own_rows, channels = all_picked.shape
+    rows = block_out.shape[0]
+    part = head.shape[1]
+    dma = pltpu.SemaphoreType.DMA
+    return pl.pallas_call(
+        functools.partial(middle_kernel, count, pairs),
+        out_shape=(
+            jax.ShapeDtypeStruct((rows, channels), BF),
+            jax.ShapeDtypeStruct((count, rows, channels // count), BF),
+        ),
+        in_specs=[vmem()] * 9,
+        out_specs=(vmem(),) * 2,
+        scratch_shapes=[
+            pltpu.VMEM((rows, channels), BF),
+            pltpu.VMEM((channels, channels), BF),
+            pltpu.VMEM((2, pairs * own_rows, part), BF),
+            pltpu.VMEM((pairs, own_rows, channels), BF),
+            pltpu.VMEM((pairs, own_rows, channels), BF),
+            pltpu.VMEM((own_rows, channels), BF),
+            pltpu.VMEM((count, own_rows, channels), BF),
+            pltpu.VMEM((rows, channels), BF),
+            dma,
+            dma,
+            dma((pairs,)),
+            dma((pairs,)),
+            dma((count,)),
+            dma((count,)),
+        ],
+        compiler_params=pltpu.CompilerParams(
+            collective_id=3, has_side_effects=True, vmem_limit_bytes=48 * 1024 * 1024
+        ),
+    )(
+        block_out, all_picked, head, other, goals, sums, hits,
+        perm.reshape(1, channels), perm.reshape(channels, 1),
+    )
+
+
 def per_device(
     features,
     norm_gain,
@@ -535,43 +559,15 @@
     conv_sum, active, block_out, all_picked, arrived = front(
         features[0], norm_gain, taps, out_weight, hits, jnp.concatenate([pieces, counted], axis=2)
     )
-    track_target = arrived[:, :, : 2 * part]
-    track_count = arrived[:, :, 2 * part : 2 * part + 1].astype(jnp.int32)
-    partner = lax.ppermute(
-        block_out, "bins", [(i, bin_devices - 1 - i) for i in range(bin_devices)]
-    )
-    all_picked = all_picked.reshape(pairs * own_rows, channels)
-
-    logits = jnp.concatenate([dot(all_picked, head_weight), dot(all_picked, other_head)], axis=1)
-    logits = logits.reshape(pairs, own_genes, exons, 2 * part)
-    predicted = jax.nn.softplus(logits).astype(BF).astype(F32)
-    counts = lax.broadcasted_iota(jnp.int32, (1, 1, exons, 1), 2) < track_count[..., None]
-    partial = jnp.sum(jnp.where(counts, predicted, 0.0), axis=2)
-    spread = (1.0 - track_target / (1.0 + partial)).astype(BF).astype(F32)
-    logit_grad = jnp.where(counts, spread[:, :, None, :] * jax.nn.sigmoid(logits), 0.0).astype(BF)
-    logit_grad = logit_grad.reshape(pairs * own_rows, 2 * part)
-    picked_grad = dot(logit_grad[:, :part], head_weight, ((1,), (1,))) + dot(
-        logit_grad[:, part:], other_head, ((1,), (1,))
-    )
-    picked_grad = picked_grad.astype(BF).reshape(pairs, own_rows, channels)
-    own_grad = reduce_pieces(picked_grad, "batch", 4, 2)
-    seq_grad = gather(own_grad, "bins", 5).reshape(genes * exons, channels)
-    head_back = dot(hits, seq_grad, ((0,), (0,)))
-
-    flip = (
-        lax.broadcasted_iota(jnp.int32, (rows, rows), 0)
-        == rows - 1 - lax.broadcasted_iota(jnp.int32, (rows, rows), 1)
-    ).astype(BF)
-    down = lax.broadcasted_iota(jnp.int32, (channels, channels), 0)
-    along = lax.broadcasted_iota(jnp.int32, (channels, channels), 1)
-    both_maps = (
-        (down == rc_perm[None, :]).astype(F32) + (rc_perm[:, None] == along).astype(F32)
-    ).astype(BF)
-    mirrored = dot(flip, partner).astype(BF)
-    rc_grad = block_out.astype(F32) - 0.5 * dot(mirrored, both_maps)
-    block_grad = (head_back + rc_grad).astype(BF)
-
-    wide = channels // bin_devices
+    gene_rows = pairs * own_genes
+    goals = arrived[:, :, : 2 * part].reshape(gene_rows, 2 * part)
+    row_count = arrived[:, :, 2 * part].reshape(gene_rows, 1).astype(jnp.int32)
+    row = lax.broadcasted_iota(jnp.int32, (gene_rows, gene_rows * exons), 1)
+    gene = lax.broadcasted_iota(jnp.int32, (gene_rows, gene_rows * exons), 0)
+    sums = ((row // exons == gene) & (row % exons < row_count)).astype(BF)
+    block_grad, grad_parts = middle(
+        block_out, all_picked, head_weight, other_head, goals, sums, hits, rc_perm
+    )
     input_grad, own_parts = tail(
         features[0],
         norm_gain,
@@ -580,7 +576,7 @@
         conv_sum,
         active,
         block_grad,
-        block_grad.reshape(rows, bin_devices, wide).transpose(1, 0, 2),
+        grad_parts,
     )
     out_weight_grad = own_parts.transpose(1, 0, 2).reshape(hid // batch_devices, channels)
     out_weight_grad = out_weight_grad.astype(F32)

time: 138 us -> 126 us (0.913)
  waiting for transfers between devices: 17.3 us -> 0.01 us
  matrix products: 11.1 us -> 0 us
  Pallas kernels: 92.9 us -> 101 us
  local copies, waits for them, and re-layouts: 10.8 us -> 18.4 us
    ppermute x1 -> x0, waiting for transfers between devices: 17.3 us -> none  [per_device(): lax.ppermute(block_out, 'bins', [(i, bin_devices - 1 - i) for i in range(...]
    dot_general x6 -> x0, matrix products: 11.1 us -> none  [dot(): return lax.dot_general(a, b, (dims, ((), ())), preferred_element_type=F32)]
    pallas_call x2 -> x1, Pallas kernels: 19 us -> 28.3 us  [middle(): pl.pallas_call(functools.partial(middle_kernel, count, pairs), out_shape=...]
    unnamed x26 -> x30, local copies, waits for them, and re-layouts: 4.96 us -> 11.4 us
  transfers between devices with their start and end apart: 2 -> 1, of which waited for: 1 -> 0; matrix products, arithmetic and copies ran while one was open for 9% -> 7% of each run, Pallas kernels for 21% -> 23%
where the time goes in v4:
time: 126 us; the launch traced here: 124 us
  Pallas kernels  101 us (80%)
  local copies, waits for them, and re-layouts  18.4 us (15%)
  other arithmetic  3.24 us (3%)
    pallas_call x1, Pallas kernels, tail(): pl.pallas_call(functools.partial(tail_kernel, count, batch), out_shape=(j...  44.4 us
    pallas_call x1, Pallas kernels, front(): pl.pallas_call(functools.partial(front_kernel, count, pairs), out_shape=(...  28.8 us
    pallas_call x1, Pallas kernels, middle(): pl.pallas_call(functools.partial(middle_kernel, count, pairs), out_shape=...  28.3 us
    unnamed x30, local copies, waits for them, and re-layouts  11.4 us
  transfers between devices with their start and end apart: 1, of which 0 were waited for; matrix products, arithmetic and copies ran while one was open for 7% of the time, Pallas kernels for 23%

profile of v4, /device:TPU:15, one launch (start us, length us, event | category | flops | bytes accessed | tf_op | source)
XLA Modules:
  0.0 124.3 jit_solution(12114663287470513764)
XLA Ops:
  1.0 1.1 squeeze.13
  2.1 0.8 fusion.4
  2.9 1.0 fusion.3
  3.9 0.7 reshape.111.perm_row_ref
  4.6 1.0 reshape.114.perm_col_ref
  5.6 0.7 iota_compare_fusion.1
  7.1 0.8 copy.16
  8.2 0.7 compare_bitcast_fusion
  9.8 1.1 copy-done.1
  10.9 28.8 %shard_map.113 = (f32[256,768]{1,0:T(8,128)S(1)}, bf16[256,768]{1,0:T(8,128)(2,1)S(1)}, bf16[256,1536]{1,0:T(8,128)(2,1)S(1)}, bf16[4,32,1536]{2,1,0:T(8,128)(2,1)S(1)}, f32[4,4,1152]{2,1,0:T(4,128)S(1)}) custom-call(bf16[256,1536]{1,0:T(8,128)(2,1)S(1)} %bitcast.19, f32[1,1536]{1,0:T(1,128)S(1)} %reshape.108.gain_ref, bf16[3,1536,768]{2,1,0:T(8,128)(2,1)} %taps_ref.3, ...), custom_call_target="tpu_custom_call" | custom-call | tf_op jit(solution)/shard_map/pallas_call | solution.py:211
  39.8 0.9 copy-done.3
  40.6 0.9 copy-done.4
  41.5 0.7 copy-done.8
  42.3 0.8 copy-done.9
  43.4 1.4 %copy-done.2 = bf16[1536,512]{1,0:T(8,128)(2,1)S(1)} copy-done((bf16[1536,512]{1,0:T(8,128)(2,1)S(1)}, bf16[1536,512]{1,0:T(8,128)(2,1)}, u32[]{:S(2)}) %copy-start.2) | copy-done | bytes 1572888
  44.8 1.1 copy-done.5
  46.0 1.0 copy-done.10
  47.0 28.3 %shard_map.114 = (bf16[256,1536]{1,0:T(8,128)(2,1)S(1)}, bf16[4,256,384]{2,1,0:T(8,128)(2,1)S(1)}) custom-call(bf16[256,1536]{1,0:T(8,128)(2,1)S(1)} %copy-done.5, bf16[4,32,1536]{2,1,0:T(8,128)(2,1)S(1)} %copy-done.10, bf16[1536,512]{1,0:T(8,128)(2,1)S(1)} %copy-done.2, bf16[1536,512]{1,0:T(8,128)(2,1)} %collective-permute-done.other_ref, ...), custom_call_target="tpu_custom_call" | custom-call | tf_op jit(solution)/shard_map/pallas_call | solution.py:483
  75.3 0.9 copy-done.6
  76.1 0.9 copy-done.7
  77.0 44.4 %shard_map.115 = (bf16[256,1536]{1,0:T(8,128)(2,1)}, bf16[4,96,384]{2,1,0:T(8,128)(2,1)}) custom-call(bf16[256,1536]{1,0:T(8,128)(2,1)} %bitcast.18, f32[1,1536]{1,0:T(1,128)} %copy-done.11, bf16[3,1536,768]{2,1,0:T(8,128)(2,1)} %taps_ref.3, bf16[768,1536]{1,0:T(8,128)(2,1)} %ow_ref.3, f32[256,768]{1,0:T(8,128)} %copy-done.3, bf16[256,768]{1,0:T(8,128)(2,1)} %copy-done.8, ...), custom_call_target="tpu_custom_call" | custom-call | tf_op jit(solution)/shard_map/pallas_call | solution.py:362
  121.5 1.1 convert_bitcast_fusion
  122.5 0.9 copy.22
  123.4 0.9 copy.27
  (45 shorter events, 2.6 us)
Async XLA Ops:
  0.6 8.8 %copy-start.13 = (s32[1,16]{1,0:T(1,128)S(1)}, s32[1,16]{1,0:T(1,128)}, u32[]{:S(2)}) copy-start(s32[1,16]{1,0:T(1,128)} %param.17) | copy-start | bytes 196
  0.6 9.1 %copy-start = (bf16[768,1536]{1,0:T(8,128)(2,1)S(1)}, bf16[768,1536]{1,0:T(8,128)(2,1)}, u32[]{:S(2)}) copy-start(bf16[768,1536]{1,0:T(8,128)(2,1)} %ow_ref.3) | copy-start | bytes 7077892
  0.7 42.8 %collective-permute-start = (bf16[1536,512]{1,0:T(8,128)(2,1)}, bf16[1536,512]{1,0:T(8,128)(2,1)}, u32[]{:S(2)}, u32[]{:S(2)}) collective-permute-start(bf16[1536,512]{1,0:T(8,128)(2,1)} %head_ref.1), channel_id=1, source_target_pairs={{0,1},{1,0},{2,3},{3,2},{4,5},{5,4},{6,7},{7,6},{8,9},{9,8},{10,11... | collective-permute-start | bytes 4718600 | tf_op jit(solution)/shard_map/ppermute | solution.py:539
  7.1 32.6 %copy-start.11 = (f32[1,1536]{1,0:T(1,128)}, f32[1,1536]{1,0:T(1,128)S(1)}, u32[]{:S(2)}) copy-start(f32[1,1536]{1,0:T(1,128)S(1)} %reshape.108.gain_ref) | copy-start | bytes 18436
  9.8 1.1 copy-start.1
  39.7 0.9 copy-start.3
  40.6 0.9 copy-start.4
  41.5 0.7 copy-start.8
  42.3 0.8 copy-start.9
  43.4 1.4 %copy-start.2 = (bf16[1536,512]{1,0:T(8,128)(2,1)S(1)}, bf16[1536,512]{1,0:T(8,128)(2,1)}, u32[]{:S(2)}) copy-start(bf16[1536,512]{1,0:T(8,128)(2,1)} %head_ref.1) | copy-start | bytes 4718596
  44.8 1.1 copy-start.5
  46.0 1.0 copy-start.10
  75.2 0.9 copy-start.6
  76.1 0.9 copy-start.7
  121.4 2.0 %copy-start.12 = (bf16[256,1536]{1,0:T(8,128)(2,1)S(1)}, bf16[256,1536]{1,0:T(8,128)(2,1)}, u32[]{:S(2)}) copy-start(bf16[256,1536]{1,0:T(8,128)(2,1)} %get-tuple-element.18) | copy-start | bytes 2359300

commit v5 on v4

--- a/solution.py
+++ b/solution.py
@@ -234,7 +234,7 @@
             dma((pairs,)),
         ],
         compiler_params=pltpu.CompilerParams(
-            collective_id=1, has_side_effects=True, vmem_limit_bytes=48 * 1024 * 1024
+            collective_id=1, has_side_effects=True, vmem_limit_bytes=20 * 1024 * 1024
         ),
     )(features, gain.reshape(1, channels), taps, out_weight, hits, goals)
 
@@ -382,7 +382,7 @@
         + [dma((batch,)) for _ in range(2)]
         + [dma((count,)) for _ in range(2)],
         compiler_params=pltpu.CompilerParams(
-            collective_id=6, has_side_effects=True, vmem_limit_bytes=56 * 1024 * 1024
+            collective_id=6, has_side_effects=True, vmem_limit_bytes=28 * 1024 * 1024
         ),
     )(features, gain.reshape(1, channels), taps, out_weight, conv_sum, active, grad, parts)
 
@@ -505,7 +505,7 @@
             dma((count,)),
         ],
         compiler_params=pltpu.CompilerParams(
-            collective_id=3, has_side_effects=True, vmem_limit_bytes=48 * 1024 * 1024
+            collective_id=3, has_side_effects=True, vmem_limit_bytes=20 * 1024 * 1024
         ),
     )(
         block_out, all_picked, head, other, goals, sums, hits,

time: 126 us -> 120 us (0.952)
  Pallas kernels: 101 us -> 92.8 us
  local copies, waits for them, and re-layouts: 18.4 us -> 22.6 us
    pallas_call x1, Pallas kernels: 44.4 us -> 38.6 us  [tail(): pl.pallas_call(functools.partial(tail_kernel, count, batch), out_shape=(j...]
    unnamed x30 -> x32, local copies, waits for them, and re-layouts: 11.4 us -> 15.6 us
    pallas_call x1, Pallas kernels: 28.8 us -> 25.8 us  [front(): pl.pallas_call(functools.partial(front_kernel, count, pairs), out_shape=(...]
  transfers between devices with their start and end apart: 1 -> 1, of which waited for: 0 -> 0; matrix products, arithmetic and copies ran while one was open for 7% -> 8% of each run, Pallas kernels for 23% -> 22%
where the time goes in v5:
time: 120 us; the launch traced here: 119 us
  Pallas kernels  92.8 us (77%)
  local copies, waits for them, and re-layouts  22.6 us (19%)
  other arithmetic  2.21 us (2%)
    pallas_call x1, Pallas kernels, tail(): pl.pallas_call(functools.partial(tail_kernel, count, batch), out_shape=(j...  38.6 us
    pallas_call x1, Pallas kernels, middle(): pl.pallas_call(functools.partial(middle_kernel, count, pairs), out_shape=...  28.4 us
    pallas_call x1, Pallas kernels, front(): pl.pallas_call(functools.partial(front_kernel, count, pairs), out_shape=(...  25.8 us
    unnamed x32, local copies, waits for them, and re-layouts  15.6 us
  transfers between devices with their start and end apart: 1, of which 0 were waited for; matrix products, arithmetic and copies ran while one was open for 8% of the time, Pallas kernels for 22%

profile of v5, /device:TPU:15, one launch (start us, length us, event | category | flops | bytes accessed | tf_op | source)
XLA Modules:
  0.0 118.8 jit_solution(6299819026523385358)
XLA Ops:
  1.0 1.1 squeeze.13
  2.1 0.8 fusion.4
  2.9 1.0 fusion.3
  3.9 0.7 reshape.111.perm_row_ref
  4.6 1.0 reshape.114.perm_col_ref
  5.6 0.7 iota_compare_fusion.1
  6.4 0.7 reshape.108.gain_ref
  7.1 0.8 copy.16
  8.2 0.7 compare_bitcast_fusion
  9.8 3.0 %copy-done = bf16[3,1536,768]{2,1,0:T(8,128)(2,1)S(1)} copy-done((bf16[3,1536,768]{2,1,0:T(8,128)(2,1)S(1)}, bf16[3,1536,768]{2,1,0:T(8,128)(2,1)}, u32[]{:S(2)}) %copy-start) | copy-done | bytes 7077912
  12.8 1.1 copy-done.3
  13.9 25.8 %shard_map.113 = (f32[256,768]{1,0:T(8,128)S(1)}, bf16[256,768]{1,0:T(8,128)(2,1)S(1)}, bf16[256,1536]{1,0:T(8,128)(2,1)S(1)}, bf16[4,32,1536]{2,1,0:T(8,128)(2,1)S(1)}, f32[4,4,1152]{2,1,0:T(4,128)S(1)}) custom-call(bf16[256,1536]{1,0:T(8,128)(2,1)S(1)} %bitcast.18, f32[1,1536]{1,0:T(1,128)S(1)} %reshape.108.gain_ref, bf16[3,1536,768]{2,1,0:T(8,128)(2,1)S(1)} %copy-done, ...), custom_call_target="tpu_custom_call" | custom-call | tf_op jit(solution)/shard_map/pallas_call | solution.py:211
  39.8 0.9 copy-done.6
  40.6 0.9 copy-done.8
  41.5 0.7 copy-done.10
  42.3 0.8 copy-done.12
  43.4 1.4 %copy-done.5 = bf16[1536,512]{1,0:T(8,128)(2,1)S(1)} copy-done((bf16[1536,512]{1,0:T(8,128)(2,1)S(1)}, bf16[1536,512]{1,0:T(8,128)(2,1)}, u32[]{:S(2)}) %copy-start.5) | copy-done | bytes 1572888
  44.8 1.1 copy-done.9
  45.9 1.0 copy-done.13
  46.9 28.4 %shard_map.114 = (bf16[256,1536]{1,0:T(8,128)(2,1)S(1)}, bf16[4,256,384]{2,1,0:T(8,128)(2,1)S(1)}) custom-call(bf16[256,1536]{1,0:T(8,128)(2,1)S(1)} %copy-done.9, bf16[4,32,1536]{2,1,0:T(8,128)(2,1)S(1)} %copy-done.13, bf16[1536,512]{1,0:T(8,128)(2,1)S(1)} %copy-done.5, bf16[1536,512]{1,0:T(8,128)(2,1)} %collective-permute-done.other_ref, ...), custom_call_target="tpu_custom_call" | custom-call | tf_op jit(solution)/shard_map/pallas_call | solution.py:483
  75.4 3.0 %copy-done.1 = bf16[3,1536,768]{2,1,0:T(8,128)(2,1)S(1)} copy-done((bf16[3,1536,768]{2,1,0:T(8,128)(2,1)S(1)}, bf16[3,1536,768]{2,1,0:T(8,128)(2,1)}, u32[]{:S(2)}) %copy-start.1) | copy-done | bytes 7077912
  78.4 38.6 %shard_map.115 = (bf16[256,1536]{1,0:T(8,128)(2,1)S(1)}, bf16[4,96,384]{2,1,0:T(8,128)(2,1)S(1)}) custom-call(bf16[256,1536]{1,0:T(8,128)(2,1)S(1)} %bitcast.19, f32[1,1536]{1,0:T(1,128)S(1)} %reshape.108.gain_ref, bf16[3,1536,768]{2,1,0:T(8,128)(2,1)S(1)} %copy-done.1, bf16[768,1536]{1,0:T(8,128)(2,1)S(1)} %copy-done.2, f32[256,768]{1,0:T(8,128)S(1)} %copy-done.7, ...), custom_call_target="tpu_custom_call" | custom-call | tf_op jit(solution)/shard_map/pallas_call | solution.py:362
  117.1 0.9 copy.22
  117.9 0.9 copy.27
  (47 shorter events, 2.0 us)
Async XLA Ops:
  0.6 8.8 %copy-start.14 = (s32[1,16]{1,0:T(1,128)S(1)}, s32[1,16]{1,0:T(1,128)}, u32[]{:S(2)}) copy-start(s32[1,16]{1,0:T(1,128)} %param.17) | copy-start | bytes 196
  0.6 9.1 %copy-start.2 = (bf16[768,1536]{1,0:T(8,128)(2,1)S(1)}, bf16[768,1536]{1,0:T(8,128)(2,1)}, u32[]{:S(2)}) copy-start(bf16[768,1536]{1,0:T(8,128)(2,1)} %ow_ref.3) | copy-start | bytes 7077892
  0.7 42.7 %collective-permute-start = (bf16[1536,512]{1,0:T(8,128)(2,1)}, bf16[1536,512]{1,0:T(8,128)(2,1)}, u32[]{:S(2)}, u32[]{:S(2)}) collective-permute-start(bf16[1536,512]{1,0:T(8,128)(2,1)} %head_ref.1), channel_id=1, source_target_pairs={{0,1},{1,0},{2,3},{3,2},{4,5},{5,4},{6,7},{7,6},{8,9},{9,8},{10,11... | collective-permute-start | bytes 4718600 | tf_op jit(solution)/shard_map/ppermute | solution.py:539
  9.8 3.0 %copy-start = (bf16[3,1536,768]{2,1,0:T(8,128)(2,1)S(1)}, bf16[3,1536,768]{2,1,0:T(8,128)(2,1)}, u32[]{:S(2)}) copy-start(bf16[3,1536,768]{2,1,0:T(8,128)(2,1)} %taps_ref.3) | copy-start | bytes 21233668
  12.8 1.1 copy-start.3
  39.7 0.9 copy-start.6
  40.6 0.9 copy-start.8
  41.5 0.7 copy-start.10
  42.2 0.8 copy-start.12
  43.4 1.4 %copy-start.5 = (bf16[1536,512]{1,0:T(8,128)(2,1)S(1)}, bf16[1536,512]{1,0:T(8,128)(2,1)}, u32[]{:S(2)}) copy-start(bf16[1536,512]{1,0:T(8,128)(2,1)} %head_ref.1) | copy-start | bytes 4718596
  44.8 1.1 copy-start.9
  45.9 1.0 copy-start.13
  46.9 28.4 %copy-start.4 = (bf16[1,256,1536]{2,1,0:T(8,128)(2,1)S(1)}, bf16[1,256,1536]{2,1,0:T(8,128)(2,1)}, u32[]{:S(2)}) copy-start(bf16[1,256,1536]{2,1,0:T(8,128)(2,1)} %param.10) | copy-start | bytes 2359300
  46.9 28.4 %copy-start.7 = (f32[256,768]{1,0:T(8,128)S(1)}, f32[256,768]{1,0:T(8,128)}, u32[]{:S(2)}) copy-start(f32[256,768]{1,0:T(8,128)} %copy-done.6) | copy-start | bytes 2359300
  46.9 28.4 %copy-start.11 = (bf16[256,768]{1,0:T(8,128)(2,1)S(1)}, bf16[256,768]{1,0:T(8,128)(2,1)}, u32[]{:S(2)}) copy-start(bf16[256,768]{1,0:T(8,128)(2,1)} %copy-done.10) | copy-start | bytes 1179652
  75.4 3.0 %copy-start.1 = (bf16[3,1536,768]{2,1,0:T(8,128)(2,1)S(1)}, bf16[3,1536,768]{2,1,0:T(8,128)(2,1)}, u32[]{:S(2)}) copy-start(bf16[3,1536,768]{2,1,0:T(8,128)(2,1)} %taps_ref.3) | copy-start | bytes 21233668
